TPU v7x, 128 devices: a whole 4x4x4 slice. The times are simulated.
128 devices in a mesh: dp: 8 (over x_lo, z), tensor: 16 (over x_hi, y, core).
Axes of the slice: x: 4 (x_hi: 2, x_lo: 2; x = x_hi * 2 + x_lo), y: 4, z: 4, core: 2. Of those that a mesh axis runs over, the one named last changes fastest.
Arguments:
- tokens: bfloat16 [8, 2048, 4096], P('dp', 'tensor'), may hold values from -1.8 to 1.8
- cotangent: bfloat16 [8, 2048, 4096], P('dp', None, 'tensor'), may hold values from -6 to 6
- gain: float32 [4096], replicated, may hold values from 0.25 to 3.5
- w_query: bfloat16 [4096, 4096], P(None, 'tensor'), may hold values from -6 to 6
- w_key: bfloat16 [4096, 512], P(None, 'tensor'), may hold values from -6 to 6
- w_value: bfloat16 [4096, 512], P(None, 'tensor'), may hold values from -6 to 6
- moment_query: float32 [4096, 4096], P('dp', 'tensor'), may hold values from -6 to 6
- moment_key: float32 [4096, 512], P('dp', 'tensor'), may hold values from -6 to 6
- moment_value: float32 [4096, 512], P('dp', 'tensor'), may hold values from -6 to 6
Outputs:
- attended: bfloat16 [8, 2048, 4096], P('dp', None, 'tensor')
- grad_tokens: bfloat16 [8, 2048, 4096], P('dp', 'tensor')
- fresh_query: bfloat16 [4096, 4096], P(None, 'tensor')
- fresh_key: bfloat16 [4096, 512], P(None, 'tensor')
- fresh_value: bfloat16 [4096, 512], P(None, 'tensor')
- next_query: float32 [4096, 4096], P('dp', 'tensor')
- next_key: float32 [4096, 512], P('dp', 'tensor')
- next_value: float32 [4096, 512], P('dp', 'tensor')
All inputs are finite; a program needn't handle non-finite values.
Results may differ from a plain program's by a relative error of at most 0.017.
Values may be sent and summed in bfloat16 or wider, within the bound.
A program may use at most 256 MiB of HBM per device.

v0:
```python
import jax
import jax.numpy as jnp
from jax import lax
from jax.sharding import Mesh
from jax.sharding import PartitionSpec as P

D = 4096
HEADS = 32
KVH = 4
HD = 128
TENSOR = ("tensor_0", "tensor_1", "tensor_2")
DP = ("dp_0", "dp_1")
DP_TENSOR = ("dp_0", "dp_1", "tensor_0", "tensor_1", "tensor_2")


rope_base = 1000000.0
norm_eps = 1e-06
stat_eps = 1e-06
learn_rate = 0.05
keep_rate = 0.9


def partner_2(shard, axis, distance):
    return lax.ppermute(shard, axis, [(i, i ^ 1 << distance) for i in range(lax.axis_size(axis))])


def in_blocks(shard, dim, size):
    lengths = shard.shape
    pieces = shard.reshape(*lengths[:dim], size, lengths[dim] // size, *lengths[dim + 1 :])
    return jnp.moveaxis(pieces, dim, 0)


def summed_rows(shard, chips, core, dim):
    sizes = (lax.axis_size(chips), lax.axis_size(core))
    pieces = in_blocks(shard, dim, sizes[0] * sizes[1])
    inside = pieces.shape[1:]
    pieces = pieces.reshape(*sizes, *inside).swapaxes(0, 1).reshape(-1, *inside)
    pieces = lax.psum_scatter(pieces, core, scatter_dimension=0, tiled=True)
    return lax.psum_scatter(pieces, chips, scatter_dimension=0, tiled=True)[0]


def side_by_side(arrays, axis, dim, along):
    both = jnp.concatenate(arrays, axis=along)
    out, at, done = (lax.psum_scatter(both, axis, scatter_dimension=dim, tiled=True), 0, [])
    for a in arrays:
        done.append(lax.slice_in_dim(out, at, at + a.shape[along], axis=along))
        at += a.shape[along]
    return tuple(done)


def one_axis_at_a_time(shard, axes):
    for axis in axes:
        shard = lax.psum(shard, axis)
    return shard


def in_one_piece(arrays, axis, dim, along):
    ends, at = ([], 0)
    for a in arrays[:-1]:
        at += a.shape[along]
        ends.append(at)
    both = jnp.concatenate(arrays, axis=along)
    return tuple(jnp.split(lax.all_gather(both, axis, axis=dim, tiled=True), ends, axis=along))


def rotate(matrix, first_column, head_size, sign):
    length = matrix.shape[0]
    columns = matrix.shape[1]
    index = first_column + jnp.arange(columns, dtype=jnp.int32)
    within = index % head_size // 2
    rates = jnp.power(jnp.float32(rope_base), within.astype(jnp.float32) * (-2.0 / head_size))
    angle = jnp.arange(length, dtype=jnp.float32)[:, None] * rates[None, :]
    even = index % 2 == 0
    partner = jnp.where(even[None, :], -jnp.roll(matrix, -1, axis=1), jnp.roll(matrix, 1, axis=1))
    return matrix * jnp.cos(angle) + partner * (sign * jnp.sin(angle))


def per_device(
    tokens, cotangent, gain, w_query, w_key, w_value, moment_query, moment_key, moment_value
):
    rank = lax.axis_index(TENSOR)
    query_width = w_query.shape[1]
    key_width = w_key.shape[1]
    local_heads = query_width // HD
    width = tokens.shape[2]
    in_scale = width ** (-0.5)
    head_scale = HD ** (-0.5)
    inputs = tokens[0].astype(jnp.float32)
    reciprocal = lax.rsqrt(jnp.mean(inputs * inputs, axis=1, keepdims=True) + norm_eps)
    unit_rows = inputs * reciprocal
    normed = (unit_rows * gain).astype(jnp.bfloat16)
    normed_all = lax.all_gather(normed, TENSOR, axis=0, tiled=True)
    length = normed_all.shape[0]
    query = rotate(
        jnp.dot(normed_all, w_query, preferred_element_type=jnp.float32) * in_scale,
        rank * query_width,
        HD,
        1.0,
    ).astype(jnp.bfloat16)
    key_part = rotate(
        jnp.dot(normed_all, w_key, preferred_element_type=jnp.float32) * in_scale,
        rank * key_width,
        HD,
        1.0,
    ).astype(jnp.bfloat16)
    value_part = (
        jnp.dot(normed_all, w_value, preferred_element_type=jnp.float32) * in_scale
    ).astype(jnp.bfloat16)
    span = lax.axis_size(TENSOR) // KVH
    levels = span.bit_length() - 1
    paired = jnp.stack([key_part, value_part])
    for level in range(levels):
        other = partner_2(paired, TENSOR, level)
        higher = rank // 2**level % 2 == 1
        paired = jnp.where(
            higher,
            jnp.concatenate([other, paired], axis=2),
            jnp.concatenate([paired, other], axis=2),
        )
    key_head = paired[0]
    value_head = paired[1]
    query_heads = query.reshape(length, local_heads, HD)
    grad_heads = cotangent[0].reshape(length, local_heads, HD)
    rows_block = 512
    starts = jnp.arange(length // rows_block, dtype=jnp.int32) * rows_block
    places = jnp.arange(length)

    def attend(carry, start):
        query_rows = lax.dynamic_slice_in_dim(query_heads, start, rows_block, 0)
        grad_rows = lax.dynamic_slice_in_dim(grad_heads, start, rows_block, 0)
        scores = (
            jnp.einsum("shd,td->hst", query_rows, key_head, preferred_element_type=jnp.float32)
            * head_scale
        )
        row_places = start + jnp.arange(rows_block)
        causal = row_places[:, None] >= places[None, :]
        attention = jax.nn.softmax(jnp.where(causal[None], scores, -1e30), axis=2)
        attention_low = attention.astype(jnp.bfloat16)
        attended_rows = jnp.einsum(
            "hst,td->shd", attention_low, value_head, preferred_element_type=jnp.float32
        ).astype(jnp.bfloat16)
        grad_raw = jnp.einsum(
            "shd,td->hst", grad_rows, value_head, preferred_element_type=jnp.float32
        )
        grad_scores = attention * (grad_raw - jnp.sum(attention * grad_raw, axis=2, keepdims=True))
        grad_low = (grad_scores * head_scale).astype(jnp.bfloat16)
        query_grad_rows = jnp.einsum(
            "hst,td->shd", grad_low, key_head, preferred_element_type=jnp.float32
        )
        key_term = jnp.einsum(
            "hst,shd->td", grad_low, query_rows, preferred_element_type=jnp.float32
        )
        value_term = jnp.einsum(
            "hst,shd->td", attention_low, grad_rows, preferred_element_type=jnp.float32
        )
        return ((carry[0] + key_term, carry[1] + value_term), (attended_rows, query_grad_rows))

    empty = jnp.zeros((length, HD), jnp.float32)
    (key_local, value_local), (attended_blocks, query_blocks) = lax.scan(
        attend, (empty, empty), starts
    )
    attended = attended_blocks.reshape(length, query_width)
    grad_query_raw = query_blocks.reshape(length, query_width)
    current = lax.optimization_barrier(
        jnp.stack([key_local, value_local]).astype(jnp.bfloat16)
    ).astype(jnp.float32)
    for level in reversed(range(levels)):
        middle = current.shape[2] // 2
        higher = rank // 2**level % 2 == 1
        outgoing = jnp.where(higher, current[:, :, :middle], current[:, :, middle:])
        retained = jnp.where(higher, current[:, :, middle:], current[:, :, :middle])
        current = retained + partner_2(outgoing.astype(jnp.bfloat16), TENSOR, level).astype(
            outgoing.dtype
        )
    grad_key = rotate(current[0], rank * key_width, HD, -1.0).astype(jnp.bfloat16)
    grad_value = current[1].astype(jnp.bfloat16)
    grad_query = rotate(grad_query_raw, rank * query_width, HD, -1.0).astype(jnp.bfloat16)

    def product(grad, weight):
        return jnp.einsum("sc,dc->sd", grad, weight, preferred_element_type=jnp.float32)

    grad_normed = summed_rows(
        (
            (product(grad_query, w_query) + product(grad_key, w_key) + product(grad_value, w_value))
            * in_scale
        ).astype(jnp.bfloat16),
        ("tensor_0", "tensor_1"),
        "tensor_2",
        0,
    ).astype(jnp.float32)
    grad_unit = grad_normed * gain
    inner = jnp.mean(grad_unit * unit_rows, axis=1, keepdims=True)
    grad_tokens = (reciprocal * (grad_unit - unit_rows * inner)).astype(jnp.bfloat16)[None]
    grad_wq = (
        jnp.einsum("sd,sc->dc", normed_all, grad_query, preferred_element_type=jnp.float32)
        * in_scale
    )
    grad_wk = (
        jnp.einsum("sd,sc->dc", normed_all, grad_key, preferred_element_type=jnp.float32) * in_scale
    )
    grad_wv = (
        jnp.einsum("sd,sc->dc", normed_all, grad_value, preferred_element_type=jnp.float32)
        * in_scale
    )
    summed_query, summed_key, summed_value = tuple(
        (
            part.astype(jnp.float32)
            for part in side_by_side(
                (
                    grad_wq.astype(jnp.bfloat16),
                    grad_wk.astype(jnp.bfloat16),
                    grad_wv.astype(jnp.bfloat16),
                ),
                DP,
                0,
                1,
            )
        )
    )
    square = (
        jnp.sum(summed_query * summed_query)
        + jnp.sum(summed_key * summed_key)
        + jnp.sum(summed_value * summed_value)
    )
    total = one_axis_at_a_time(square, DP_TENSOR)
    count_all = 1.0 * D * HD * (HEADS + 2 * KVH)
    factor = lax.rsqrt(total / count_all + stat_eps)
    dp_rank = lax.axis_index(DP)

    def advance(weight_own, moment, summed):
        moved = keep_rate * moment + summed * factor
        return ((weight_own.astype(jnp.float32) - learn_rate * moved).astype(jnp.bfloat16), moved)

    share = moment_query.shape[0]
    own_query = lax.dynamic_slice_in_dim(w_query, dp_rank * share, share, 0)
    own_key = lax.dynamic_slice_in_dim(w_key, dp_rank * share, share, 0)
    own_value = lax.dynamic_slice_in_dim(w_value, dp_rank * share, share, 0)
    part_query, next_query = advance(own_query, moment_query, summed_query)
    part_key, next_key = advance(own_key, moment_key, summed_key)
    part_value, next_value = advance(own_value, moment_value, summed_value)
    fresh_query, fresh_key, fresh_value = in_one_piece((part_query, part_key, part_value), DP, 0, 1)
    return (
        attended[None],
        grad_tokens,
        fresh_query,
        fresh_key,
        fresh_value,
        next_query,
        next_key,
        next_value,
    )


def solution(mesh):
    torus = Mesh(
        mesh.devices.reshape(2, 4, 2, 4, 2), ("dp_0", "dp_1", "tensor_0", "tensor_1", "tensor_2")
    )
    placed = (
        P(DP, TENSOR, None),
        P(DP, None, TENSOR),
        P(),
        P(None, TENSOR),
        P(None, TENSOR),
        P(None, TENSOR),
        P(DP, TENSOR),
        P(DP, TENSOR),
        P(DP, TENSOR),
    )
    return jax.shard_map(
        per_device,
        mesh=torus,
        in_specs=placed,
        out_specs=(
            P(DP, None, TENSOR),
            P(DP, TENSOR, None),
            P(None, TENSOR),
            P(None, TENSOR),
            P(None, TENSOR),
            P(DP, TENSOR),
            P(DP, TENSOR),
            P(DP, TENSOR),
        ),
        check_vma=False,
    )
```

profile of v0, /device:TPU:0, one launch (start us, length us, event | category | flops | bytes accessed | tf_op | source)
XLA Modules:
  0.0 772.3 jit_solution(11540395952958526187)
XLA Ops:
  13.9 110.0 %all-gather.3.cloned.1.call-done = bf16[2048,4096]{1,0:T(8,128)(2,1)} async-done(((bf16[128,4096]{1,0:T(8,128)(2,1)}), bf16[2048,4096]{1,0:T(8,128)(2,1)}) %all-gather.3.cloned.1.call-update) | async-done | bytes 16777232 | tf_op jit(solution)/shard_map/all_gather | solution.py:92
  123.9 10.9 %convolution_multiply_fusion.5 = f32[2048,32]{0,1:T(8,128)S(1)} fusion(bf16[2048,4096]{1,0:T(8,128)(2,1)} %all-gather.3.cloned.1.call-done, bf16[4096,32]{0,1:T(8,128)(2,1)S(1)} %copy-done.11), kind=kOutput, calls=%fused_computation.75 | convolution fusion | flops 536936448 | bytes 17301504 | tf_op jit(solution)/shard_map/dot_general | solution.py:101
  154.8 10.3 %fusion.83 = bf16[2048,256]{0,1:T(8,128)(2,1)} fusion(f32[2048,1]{0,1:T(1,128)S(1)} %get-tuple-element.180, f32[2048,255]{0,1:T(8,128)S(1)} %get-tuple-element.182, f32[2048,255]{0,1:T(8,128)S(1)} %get-tuple-element.181, f32[2048,1]{0,1:T(1,128)S(1)} %get-tuple-element.179, f32[2048,256]{0,1:T(8,128)S(1)} %copy-done.4, f32[256]{0:T(256)S(1)} %multiply_power_fusion, ...), kind=kLoop, calls=%fused_computation.90 | loop fusion | flops 4718592 | bytes 7341312 | tf_op jit(solution)/shard_map/convert_element_type | solution.py:99
  171.1 280.0 %while.17 = (s32[]{:T(128)}, f32[2048,128]{1,0:T(8,128)}, f32[2048,128]{1,0:T(8,128)}, bf16[4,512,2,128]{3,2,1,0:T(2,128)(2,1)}, f32[4,512,2,128]{1,0,3,2:T(4,12...) while((s32[]{:T(128)}, f32[2048,128]{1,0:T(8,128)}, ...), condition=%wide.region_5.6_spmd.clone, body=%wide.region_1.5_spmd.clone.sunk | while | flops 3269599744 | bytes 147091824 | solution.py:159
  197.4 12.8 %fusion.183 = f32[1,512,2,128]{3,1,2,0:T(8,128)S(1)} fusion(f32[512,2,2048]{2,0,1:T(8,128)} %fusion.178, bf16[2048,128]{1,0:T(8,128)(2,1)S(1)} %copy-done.18, f32[2,512,2048]{2,1,0:T(8,128)} %get-tuple-element.258, f32[2,512]{1,0:T(2,128)S(1)} %get-tuple-element.259), kind=kOutput, calls=%fused_computation.28.clone.1 | convolution fusion | flops 551554048 | bytes 17829888 | tf_op jit(solution)/shard_map/while/body/eval_jaxpr/hst,td->shd/dot_general | solution.py:147
  210.1 19.4 %fusion.180 = f32[2048,128]{1,0:T(8,128)} fusion(f32[512,2,2048]{2,0,1:T(8,128)} %fusion.178, f32[2048,128]{1,0:T(8,128)} %get-tuple-element.274, pred[]{:T(512)S(6)} %compare.38, bf16[2048,2,128]{0,2,1:T(8,128)(2,1)} %get-tuple-element.292, s32[]{:T(128)S(6)} %select_n.260, f32[2,512,2048]{2,1,0:T(8,128)} %get-tuple-element.258, ...), kind=kOutput, calls=%fused_computation.24.clone.1 | convolution fusion | flops 552078336 | bytes 35921924 | tf_op jit(solution)/shard_map/while/body/eval_jaxpr/hst,shd->td/dot_general | solution.py:150
  229.9 11.1 %dynamic_update_slice.14 = f32[4,512,2,128]{1,0,3,2:T(4,128)} dynamic-update-slice(f32[4,512,2,128]{1,0,3,2:T(4,128)} %get-tuple-element.277, f32[1,512,2,128]{1,0,3,2:T(1,128)S(1)} %copy.66, s32[]{:T(128)S(6)} %copy.74, s32[]{:T(128)} %constant.177.clone.1..sunk, s32[]{:T(128)} %constant.177.clone.1..sunk, s32[]{:T(128)} %constant.177.clone.1..sunk) | dynamic-update-slice | bytes 1048580 | tf_op jit(solution)/shard_map/while/body/jit(dynamic_update_index_in_dim)/dynamic_update_slice | solution.py:159
  267.3 12.8 %fusion.183 = f32[1,512,2,128]{3,1,2,0:T(8,128)S(1)} fusion(f32[512,2,2048]{2,0,1:T(8,128)} %fusion.178, bf16[2048,128]{1,0:T(8,128)(2,1)S(1)} %copy-done.18, f32[2,512,2048]{2,1,0:T(8,128)} %get-tuple-element.258, f32[2,512]{1,0:T(2,128)S(1)} %get-tuple-element.259), kind=kOutput, calls=%fused_computation.28.clone.1 | convolution fusion | flops 551554048 | bytes 17829888 | tf_op jit(solution)/shard_map/while/body/eval_jaxpr/hst,td->shd/dot_general | solution.py:147
  280.1 19.4 %fusion.180 = f32[2048,128]{1,0:T(8,128)} fusion(f32[512,2,2048]{2,0,1:T(8,128)} %fusion.178, f32[2048,128]{1,0:T(8,128)} %get-tuple-element.274, pred[]{:T(512)S(6)} %compare.38, bf16[2048,2,128]{0,2,1:T(8,128)(2,1)} %get-tuple-element.292, s32[]{:T(128)S(6)} %select_n.260, f32[2,512,2048]{2,1,0:T(8,128)} %get-tuple-element.258, ...), kind=kOutput, calls=%fused_computation.24.clone.1 | convolution fusion | flops 552078336 | bytes 35921924 | tf_op jit(solution)/shard_map/while/body/eval_jaxpr/hst,shd->td/dot_general | solution.py:150
  299.8 11.1 %dynamic_update_slice.14 = f32[4,512,2,128]{1,0,3,2:T(4,128)} dynamic-update-slice(f32[4,512,2,128]{1,0,3,2:T(4,128)} %get-tuple-element.277, f32[1,512,2,128]{1,0,3,2:T(1,128)S(1)} %copy.66, s32[]{:T(128)S(6)} %copy.74, s32[]{:T(128)} %constant.177.clone.1..sunk, s32[]{:T(128)} %constant.177.clone.1..sunk, s32[]{:T(128)} %constant.177.clone.1..sunk) | dynamic-update-slice | bytes 1048580 | tf_op jit(solution)/shard_map/while/body/jit(dynamic_update_index_in_dim)/dynamic_update_slice | solution.py:159
  337.2 12.8 %fusion.183 = f32[1,512,2,128]{3,1,2,0:T(8,128)S(1)} fusion(f32[512,2,2048]{2,0,1:T(8,128)} %fusion.178, bf16[2048,128]{1,0:T(8,128)(2,1)S(1)} %copy-done.18, f32[2,512,2048]{2,1,0:T(8,128)} %get-tuple-element.258, f32[2,512]{1,0:T(2,128)S(1)} %get-tuple-element.259), kind=kOutput, calls=%fused_computation.28.clone.1 | convolution fusion | flops 551554048 | bytes 17829888 | tf_op jit(solution)/shard_map/while/body/eval_jaxpr/hst,td->shd/dot_general | solution.py:147
  350.0 19.4 %fusion.180 = f32[2048,128]{1,0:T(8,128)} fusion(f32[512,2,2048]{2,0,1:T(8,128)} %fusion.178, f32[2048,128]{1,0:T(8,128)} %get-tuple-element.274, pred[]{:T(512)S(6)} %compare.38, bf16[2048,2,128]{0,2,1:T(8,128)(2,1)} %get-tuple-element.292, s32[]{:T(128)S(6)} %select_n.260, f32[2,512,2048]{2,1,0:T(8,128)} %get-tuple-element.258, ...), kind=kOutput, calls=%fused_computation.24.clone.1 | convolution fusion | flops 552078336 | bytes 35921924 | tf_op jit(solution)/shard_map/while/body/eval_jaxpr/hst,shd->td/dot_general | solution.py:150
  369.8 11.1 %dynamic_update_slice.14 = f32[4,512,2,128]{1,0,3,2:T(4,128)} dynamic-update-slice(f32[4,512,2,128]{1,0,3,2:T(4,128)} %get-tuple-element.277, f32[1,512,2,128]{1,0,3,2:T(1,128)S(1)} %copy.66, s32[]{:T(128)S(6)} %copy.74, s32[]{:T(128)} %constant.177.clone.1..sunk, s32[]{:T(128)} %constant.177.clone.1..sunk, s32[]{:T(128)} %constant.177.clone.1..sunk) | dynamic-update-slice | bytes 1048580 | tf_op jit(solution)/shard_map/while/body/jit(dynamic_update_index_in_dim)/dynamic_update_slice | solution.py:159
  407.1 12.8 %fusion.183 = f32[1,512,2,128]{3,1,2,0:T(8,128)S(1)} fusion(f32[512,2,2048]{2,0,1:T(8,128)} %fusion.178, bf16[2048,128]{1,0:T(8,128)(2,1)S(1)} %copy-done.18, f32[2,512,2048]{2,1,0:T(8,128)} %get-tuple-element.258, f32[2,512]{1,0:T(2,128)S(1)} %get-tuple-element.259), kind=kOutput, calls=%fused_computation.28.clone.1 | convolution fusion | flops 551554048 | bytes 17829888 | tf_op jit(solution)/shard_map/while/body/eval_jaxpr/hst,td->shd/dot_general | solution.py:147
  419.9 19.4 %fusion.180 = f32[2048,128]{1,0:T(8,128)} fusion(f32[512,2,2048]{2,0,1:T(8,128)} %fusion.178, f32[2048,128]{1,0:T(8,128)} %get-tuple-element.274, pred[]{:T(512)S(6)} %compare.38, bf16[2048,2,128]{0,2,1:T(8,128)(2,1)} %get-tuple-element.292, s32[]{:T(128)S(6)} %select_n.260, f32[2,512,2048]{2,1,0:T(8,128)} %get-tuple-element.258, ...), kind=kOutput, calls=%fused_computation.24.clone.1 | convolution fusion | flops 552078336 | bytes 35921924 | tf_op jit(solution)/shard_map/while/body/eval_jaxpr/hst,shd->td/dot_general | solution.py:150
  439.7 11.1 %dynamic_update_slice.14 = f32[4,512,2,128]{1,0,3,2:T(4,128)} dynamic-update-slice(f32[4,512,2,128]{1,0,3,2:T(4,128)} %get-tuple-element.277, f32[1,512,2,128]{1,0,3,2:T(1,128)S(1)} %copy.66, s32[]{:T(128)S(6)} %copy.74, s32[]{:T(128)} %constant.177.clone.1..sunk, s32[]{:T(128)} %constant.177.clone.1..sunk, s32[]{:T(128)} %constant.177.clone.1..sunk) | dynamic-update-slice | bytes 1048580 | tf_op jit(solution)/shard_map/while/body/jit(dynamic_update_index_in_dim)/dynamic_update_slice | solution.py:159
  460.1 11.9 %fusion.87 = bf16[2048,256]{0,1:T(8,128)(2,1)S(1)} fusion(f32[2048,1]{0,1:T(1,128)S(1)} %get-tuple-element.176, f32[2048,255]{0,1:T(8,128)} %get-tuple-element.178, f32[2048,255]{0,1:T(8,128)} %get-tuple-element.177, f32[2048,1]{0,1:T(1,128)S(1)} %get-tuple-element.175, f32[2048,256]{0,1:T(8,128)} %bitcast.183, f32[256]{0:T(256)S(1)} %copy-done.25, ...), kind=kLoop, calls=%fused_computation.95 | loop fusion | flops 5242880 | bytes 7341312 | tf_op jit(solution)/shard_map/convert_element_type | solution.py:177
  488.9 13.6 %fusion.135 = f32[2048,4096]{1,0:T(8,128)} fusion(bf16[2048,32]{0,1:T(8,128)(2,1)S(1)} %fusion.99, bf16[4096,32]{0,1:T(8,128)(2,1)S(1)} %copy-done.12), kind=kOutput, calls=%fused_computation.184 | convolution fusion | flops 536870912 | bytes 33947648 | tf_op jit(solution)/shard_map/sc,dc->sd/dot_general | solution.py:180
  502.5 13.3 %fusion.109 = f32[2048,4096]{1,0:T(8,128)} fusion(bf16[4096,32]{0,1:T(8,128)(2,1)S(1)} %copy-done.14, f32[2,2048,32]{1,2,0:T(8,128)S(1)} %convert_add_fusion.1), kind=kOutput, calls=%fused_computation.144 | convolution fusion | flops 536870912 | bytes 33947648 | tf_op jit(solution)/shard_map/sc,dc->sd/dot_general | solution.py:180
  515.8 28.9 %multiply_convert_fusion = bf16[2048,4096]{1,0:T(8,128)(2,1)} fusion(f32[2048,4096]{1,0:T(8,128)} %fusion.109, f32[2048,4096]{1,0:T(8,128)} %fusion.135, bf16[2048,256]{0,1:T(8,128)(2,1)} %copy-done.8, bf16[4096,256]{1,0:T(8,128)(2,1)S(1)} %copy-done), kind=kOutput, calls=%fused_computation.57 | convolution fusion | flops 4328521728 | bytes 87031808 | tf_op jit(solution)/shard_map/sc,dc->sd/dot_general | solution.py:180
  544.7 14.0 %copy.42 = bf16[2,8,128,4096]{3,2,1,0:T(8,128)(2,1)} copy(bf16[2,8,128,4096]{3,2,0,1:T(8,128)(2,1)} %bitcast.179) | data formatting | bytes 33554432 | tf_op jit(solution)/shard_map/transpose | solution.py:37
  569.4 11.3 %psum.36 = f32[]{:T(128)} all-reduce(f32[]{:T(128)} %psum.35), channel_id=1, replica_groups=mesh['dp_0'=2,'dp_1'=4,'tensor_0'=2,'tensor_1'=4,'tensor_2'=2] {'dp_1'}, use_global_device_ids=true, to_apply=%region_14.15 | all-reduce | flops 1 | bytes 8 | tf_op jit(solution)/shard_map/psum | solution.py:53
  610.4 33.9 %all-gather.5.cloned.1.call-done = bf16[4096,320]{0,1:T(8,128)(2,1)} async-done(((bf16[512,320]{0,1:T(8,128)(2,1)}), bf16[4096,320]{0,1:T(8,128)(2,1)}) %all-gather.5.cloned.1.call-update) | async-done | bytes 2621456 | tf_op jit(solution)/shard_map/all_gather | solution.py:63
  653.4 108.7 %reduce-scatter.6.cloned.1.call-done = bf16[1,128,4096]{2,1,0:T(8,128)(2,1)} async-done(((bf16[8,128,4096]{2,1,0:T(8,128)(2,1)}), bf16[1,128,4096]{2,1,0:T(8,128)(2,1)}) %reduce-scatter.6.cloned.1.call-update) | async-done | bytes 1048592 | tf_op jit(solution)/shard_map/reduce_scatter | solution.py:39
  (223 shorter events, 206.8 us)
Async XLA Ops:
  7.2 134.7 %copy-start = (bf16[4096,256]{1,0:T(8,128)(2,1)S(1)}, bf16[4096,256]{1,0:T(8,128)(2,1)}, u32[]{:S(2)}) copy-start(bf16[4096,256]{1,0:T(8,128)(2,1)} %param.14) | copy-start | bytes 6291460
  7.2 116.7 %all-gather.3.cloned.1.call-start = ((), (), s32[]{:S(2)}) async-start(), calls=%async_computation.3 | async-start | bytes 17825792 | tf_op jit(solution)/shard_map/all_gather | solution.py:92
  9.5 114.3 %copy-start.11 = (bf16[4096,32]{0,1:T(8,128)(2,1)S(1)}, bf16[4096,32]{0,1:T(8,128)(2,1)}, u32[]{:S(2)}) copy-start(bf16[4096,32]{0,1:T(8,128)(2,1)} %param.15) | copy-start | bytes 786436
  12.1 546.7 %reduce-scatter.8.cloned.1.call-start = ((), (), s32[]{:S(2)}) async-start(), calls=%async_computation.6 | async-start | bytes 2949120 | tf_op jit(solution)/shard_map/reduce_scatter | solution.py:44
  13.8 121.1 %copy-start.26 = (pred[32]{0:T(512)(128)(4,1)}, pred[32]{0:T(512)(128)(4,1)S(1)}, u32[]{:S(2)}) copy-start(pred[32]{0:T(512)(128)(4,1)S(1)} %fusion.113) | copy-start | bytes 100
  13.8 121.1 %copy-start.28 = (f32[32]{0:T(128)}, f32[32]{0:T(128)S(1)}, u32[]{:S(2)}) copy-start(f32[32]{0:T(128)S(1)} %multiply_power_fusion.1) | copy-start | bytes 388
  13.8 140.9 %copy-start.30 = (pred[256]{0:T(512)(128)(4,1)}, pred[256]{0:T(512)(128)(4,1)S(1)}, u32[]{:S(2)}) copy-start(pred[256]{0:T(512)(128)(4,1)S(1)} %fusion.112) | copy-start | bytes 772
  13.9 140.9 %copy-start.24 = (f32[256]{0:T(256)}, f32[256]{0:T(256)S(1)}, u32[]{:S(2)}) copy-start(f32[256]{0:T(256)S(1)} %multiply_power_fusion) | copy-start | bytes 3076
  13.9 122.4 %copy-start.13 = (bf16[4096,32]{0,1:T(8,128)(2,1)S(1)}, bf16[4096,32]{0,1:T(8,128)(2,1)}, u32[]{:S(2)}) copy-start(bf16[4096,32]{0,1:T(8,128)(2,1)} %param.16) | copy-start | bytes 786436
  141.4 13.1 %collective-permute-start = (bf16[2,2048,32]{1,2,0:T(8,128)(2,1)S(1)}, bf16[2,2048,32]{1,2,0:T(8,128)(2,1)S(1)}, u32[]{:S(2)}, u32[]{:S(2)}) collective-permute-start(bf16[2,2048,32]{1,2,0:T(8,128)(2,1)S(1)} %pad_maximum_fusion.3), channel_id=1, source_target_pairs={{0,1},{1,0},{2,3},{3,2},{4,5},{5,4},{6,7},{7,6},{8,9},{9,8},{10,11... | collective-permute-start | bytes 786440 | tf_op jit(solution)/shard_map/ppermute | solution.py:24
  154.6 14.1 %collective-permute-start.1 = (bf16[2,2048,64]{1,2,0:T(8,128)(2,1)S(1)}, bf16[2,2048,64]{1,2,0:T(8,128)(2,1)S(1)}, u32[]{:S(2)}, u32[]{:S(2)}) collective-permute-start(bf16[2,2048,64]{1,2,0:T(8,128)(2,1)S(1)} %maximum_select_fusion.1), channel_id=1, source_target_pairs={{0,2},{1,3},{2,0},{3,1},{4,6},{5,7},{6,4},{7,5},{8,10},{9,11},{10,... | collective-permute-start | bytes 1572872 | tf_op jit(solution)/shard_map/ppermute | solution.py:24
  459.2 14.1 %copy-start.2 = (bf16[2048,4096]{1,0:T(8,128)(2,1)S(1)}, bf16[2048,4096]{1,0:T(8,128)(2,1)}, u32[]{:S(2)}) copy-start(bf16[2048,4096]{1,0:T(8,128)(2,1)} %all-gather.3.cloned.1.call-done) | copy-start | bytes 50331652
  459.7 13.3 %collective-permute-start.2 = (bf16[2,2048,64]{1,2,0:T(8,128)(2,1)S(1)}, bf16[2,2048,64]{1,2,0:T(8,128)(2,1)S(1)}, u32[]{:S(2)}, u32[]{:S(2)}) collective-permute-start(bf16[2,2048,64]{1,2,0:T(8,128)(2,1)S(1)} %select_convert_fusion), channel_id=1, source_target_pairs={{0,2},{1,3},{2,0},{3,1},{4,6},{5,7},{6,4},{7,5},{8,10},{9,11},{10,... | collective-permute-start | bytes 1572872 | tf_op jit(solution)/shard_map/ppermute | solution.py:24
  473.3 4.9 collective-permute-start.3
  487.9 14.6 %copy-start.14 = (bf16[4096,32]{0,1:T(8,128)(2,1)S(1)}, bf16[4096,32]{0,1:T(8,128)(2,1)}, u32[]{:S(2)}) copy-start(bf16[4096,32]{0,1:T(8,128)(2,1)} %param.16) | copy-start | bytes 786436
  487.9 118.5 %reduce-scatter.4.cloned.1.call-start = ((), (), s32[]{:S(2)}) async-start(), calls=%async_computation.4 | async-start | bytes 25165824 | tf_op jit(solution)/shard_map/reduce_scatter | solution.py:38
  558.7 44.2 %copy-start.20 = (f32[512,32]{0,1:T(8,128)S(1)}, f32[512,32]{0,1:T(8,128)}, u32[]{:S(2)}) copy-start(f32[512,32]{0,1:T(8,128)} %param.18) | copy-start | bytes 196612
  558.7 44.2 %copy-start.21 = (f32[512,32]{0,1:T(8,128)S(1)}, f32[512,32]{0,1:T(8,128)}, u32[]{:S(2)}) copy-start(f32[512,32]{0,1:T(8,128)} %param.19) | copy-start | bytes 196612
  558.7 85.6 %all-gather.5.cloned.1.call-start = ((), (), s32[]{:S(2)}) async-start(), calls=%async_computation.7 | async-start | bytes 2949120 | tf_op jit(solution)/shard_map/all_gather | solution.py:63
  558.8 45.6 %copy-start.10 = (bf16[512,320]{0,1:T(8,128)(2,1)S(1)}, bf16[512,320]{0,1:T(8,128)(2,1)}, u32[]{:S(2)}) copy-start(bf16[512,320]{0,1:T(8,128)(2,1)} %reduce-scatter.8.cloned.1.call-done) | copy-start | bytes 983044
  606.3 155.8 %reduce-scatter.6.cloned.1.call-start = ((), (), s32[]{:S(2)}) async-start(), calls=%async_computation.5 | async-start | bytes 9437184 | tf_op jit(solution)/shard_map/reduce_scatter | solution.py:39
  647.4 114.7 %copy-start.6 = (bf16[1,128,4096]{2,1,0:T(8,128)(2,1)S(1)}, bf16[1,128,4096]{2,1,0:T(8,128)(2,1)}, u32[]{:S(2)}) copy-start(bf16[1,128,4096]{2,1,0:T(8,128)(2,1)} %param.11) | copy-start | bytes 3145732
  647.4 114.7 %copy-start.19 = (f32[4096]{0:T(1024)S(1)}, f32[4096]{0:T(1024)}, u32[]{:S(2)}) copy-start(f32[4096]{0:T(1024)} %param.13) | copy-start | bytes 49156
  647.4 114.7 %copy-start.23 = (f32[128]{0:T(128)S(1)}, f32[128]{0:T(128)}, u32[]{:S(2)}) copy-start(f32[128]{0:T(128)} %copy-done.22) | copy-start | bytes 1540
  (36 other events, 146.9 us)
Sparse Core Ops, SparseCore 0:
  12.3 111.5 all-gather.2
  488.1 42.4 reduce-scatter.7
  558.9 26.8 reduce-scatter.3
  606.4 37.7 all-gather.4
  648.4 113.6 reduce-scatter.5
where the time goes:
time: 781 us; the launch traced here: 772 us
  matrix products  299 us (38%)
  waiting for transfers between devices  258 us (33%)
  local copies, waits for them, and re-layouts  105 us (13%)
  other arithmetic  47.3 us (6%)
  blocking collectives  36.2 us (5%)
  between operations  17.2 us (2%)
  loops' own time  8.27 us (1%)
    all_gather x1, waiting for transfers between devices, per_device(): normed_all = lax.all_gather(normed, TENSOR, axis=0, tiled=True)  110 us
    reduce_scatter x1, waiting for transfers between devices, summed_rows(): return lax.psum_scatter(pieces, chips, scatter_dimension=0, tiled=True)[0]  109 us
    dot_general x4, matrix products, attend(): jnp.einsum('hst,shd->td', grad_low, query_rows, preferred_element_type=jn...  77.6 us
    dot_general x3, matrix products, product(): jnp.einsum('sc,dc->sd', grad, weight, preferred_element_type=jnp.float32)  55.9 us
    dot_general x4, matrix products, attend(): jnp.einsum('hst,td->shd', grad_low, key_head, preferred_element_type=jnp....  51.1 us
    dynamic_update_slice x12, local copies, waits for them, and re-layouts, per_device(): lax.scan(attend, (empty, empty), starts)  49.8 us
    psum x5, blocking collectives, one_axis_at_a_time(): shard = lax.psum(shard, axis)  36.2 us
    all_gather x1, waiting for transfers between devices, in_one_piece(): lax.all_gather(both, axis, axis=dim, tiled=True)  33.9 us
  transfers between devices with their start and end apart: 9, of which 5 were waited for; matrix products, arithmetic and copies ran while one was open for 17% of the time, Pallas kernels for 0%

commit v1 on v0

v1 whole, which is shorter than its diff:
```python
import functools

import jax
import jax.numpy as jnp
from jax import lax
from jax.experimental import pallas as pl
from jax.experimental.pallas import tpu as pltpu
from jax.sharding import Mesh
from jax.sharding import PartitionSpec as P

D = 4096
HEADS = 32
KVH = 4
HD = 128
F32 = jnp.float32
BF = jnp.bfloat16
CHIPS = ("x", "yh", "yl")
TENSOR = ("x", "yh", "yl", "core")
SHARE = ("yl", "core")
DP = ("dp_0", "dp_1")
ALL = ("dp_0", "dp_1", "x", "yh", "yl", "core")

rope_base = 1000000.0
norm_eps = 1e-06
stat_eps = 1e-06
learn_rate = 0.05
keep_rate = 0.9


def rope(x, cos, sin, sign):
    lane = lax.broadcasted_iota(jnp.int32, x.shape, 1)
    nxt = pltpu.roll(x, x.shape[1]-1, 1)
    prv = pltpu.roll(x, 1, 1)
    partner = jnp.where(lane % 2 == 0, -nxt, prv)
    return x*cos + partner*(sin*sign)

NT=(((1,),(1,)),((),()))
TN=(((0,),(0,)),((),()))
def dotg(a,b,dims):
    return lax.dot_general(a,b,dims,preferred_element_type=F32)

def attn_kernel(BQ, TC, hs, q_ref, k_ref, v_ref, do_ref, cos_ref, sin_ref,
                out_ref, gq_ref, gk_ref, gv_ref, va, s_scr, r_scr, p_scr, dk, dv, m_scr, o_scr, g_scr):
    i = pl.program_id(0)
    n = pl.num_programs(0)
    T = k_ref.shape[0]
    R = 2*BQ
    @pl.when(i == 0)
    def _():
        va[:, :HD] = v_ref[...]
        va[:, HD:] = jnp.ones((T, HD), BF)
        dk[...] = jnp.zeros_like(dk)
        dv[...] = jnp.zeros_like(dv)
    q = jnp.concatenate([q_ref[:, :HD], q_ref[:, HD:]], axis=0)
    do = jnp.concatenate([do_ref[:, :HD], do_ref[:, HD:]], axis=0)
    first = i*BQ
    full = first // TC
    used = (first + BQ + TC - 1)//TC
    m_scr[...] = jnp.full((R, HD), -3e38, F32)
    def lane_max(s):
        m = m_scr[...]
        for j in range(TC//HD):
            m = jnp.maximum(m, s[:, j*HD:(j+1)*HD])
        m_scr[...] = m
    def scores(c):
        ks = k_ref[pl.ds(pl.multiple_of(c*TC, TC), TC), :]
        vs = v_ref[pl.ds(pl.multiple_of(c*TC, TC), TC), :]
        r_scr[c] = dotg(do, vs, NT)
        return dotg(q, ks, NT)
    def body1(c, _):
        s = scores(c)
        s_scr[c] = s
        lane_max(s)
        return 0
    lax.fori_loop(0, full, body1, 0)
    def body1d(c, _):
        s = scores(c)
        row = first + lax.broadcasted_iota(jnp.int32, (R, TC), 0) % BQ
        col = c*TC + lax.broadcasted_iota(jnp.int32, (R, TC), 1)
        s = jnp.where(row >= col, s, -1e30)
        s_scr[c] = s
        lane_max(s)
        return 0
    lax.fori_loop(full, used, body1d, 0)
    c2 = hs * 1.4426950408889634
    m = jnp.max(m_scr[...], axis=1, keepdims=True)
    mb = jnp.broadcast_to(m * c2, (R, HD))
    o_scr[...] = jnp.zeros_like(o_scr)
    def body2(c, _):
        s = s_scr[c]
        p = jnp.concatenate([jnp.exp2(s[:, j*HD:(j+1)*HD]*c2 - mb) for j in range(TC//HD)], axis=1).astype(BF)
        p_scr[c] = p
        o_scr[...] += jnp.dot(p, va[pl.ds(pl.multiple_of(c*TC, TC), TC), :], preferred_element_type=F32)
        return 0
    lax.fori_loop(0, used, body2, 0)
    inv = 1.0 / o_scr[:, HD:]
    o = o_scr[:, :HD] * inv
    out_ref[:, :HD] = o[:BQ].astype(BF)
    out_ref[:, HD:] = o[BQ:].astype(BF)
    dof = do.astype(F32)
    delta = jnp.broadcast_to(jnp.sum(dof*o, axis=1, keepdims=True), (R, HD))
    qn = (q.astype(F32) * (inv*hs)).astype(BF)
    don = (dof*inv).astype(BF)
    g_scr[...] = jnp.zeros_like(g_scr)
    def body3(c, _):
        at = pl.ds(pl.multiple_of(c*TC, TC), TC)
        p = p_scr[c]
        r = r_scr[c]
        pf = p.astype(F32)
        g = jnp.concatenate([pf[:, j*HD:(j+1)*HD]*(r[:, j*HD:(j+1)*HD] - delta) for j in range(TC//HD)], axis=1).astype(BF)
        g_scr[...] += jnp.dot(g, k_ref[at, :], preferred_element_type=F32)
        dk[at, :] += dotg(g, qn, TN)
        dv[at, :] += dotg(p, don, TN)
        return 0
    lax.fori_loop(0, used, body3, 0)
    gq = g_scr[...] * (inv*hs)
    here = pl.ds(pl.multiple_of(first, BQ), BQ)
    cos = cos_ref[here, :]
    sin = sin_ref[here, :]
    gq_ref[:, :HD] = rope(gq[:BQ], cos, sin, -1.0).astype(BF)
    gq_ref[:, HD:] = rope(gq[BQ:], cos, sin, -1.0).astype(BF)
    @pl.when(i == n-1)
    def _():
        gk_ref[...] = rope(dk[...], cos_ref[...], sin_ref[...], -1.0).astype(BF)
        gv_ref[...] = dv[...].astype(BF)

def attention(q, k, v, do, cos, sin, BQ=512, TC=512):
    T = q.shape[0]
    R = 2*BQ
    whole = pl.BlockSpec((T, HD), lambda i: (0, 0))
    rows = pl.BlockSpec((BQ, 2*HD), lambda i: (i, 0))
    return pl.pallas_call(
        functools.partial(attn_kernel, BQ, TC, HD**-0.5),
        grid=(T//BQ,),
        in_specs=[rows, whole, whole, rows, whole, whole],
        out_specs=[rows, rows, whole, whole],
        out_shape=[jax.ShapeDtypeStruct((T, 2*HD), BF)]*2 + [jax.ShapeDtypeStruct((T, HD), BF)]*2,
        scratch_shapes=[pltpu.VMEM((T, 2*HD), BF), pltpu.VMEM((T//TC, R, TC), F32), pltpu.VMEM((T//TC, R, TC), F32),
            pltpu.VMEM((T//TC, R, TC), BF), pltpu.VMEM((T, HD), F32), pltpu.VMEM((T, HD), F32),
            pltpu.VMEM((R, HD), F32), pltpu.VMEM((R, 2*HD), F32), pltpu.VMEM((R, HD), F32)],
        compiler_params=pltpu.CompilerParams(vmem_limit_bytes=56*1024*1024),
        name="attention",
    )(q, k, v, do, cos, sin)


def in_blocks(shard, dim, size):
    lengths = shard.shape
    pieces = shard.reshape(*lengths[:dim], size, lengths[dim] // size, *lengths[dim + 1 :])
    return jnp.moveaxis(pieces, dim, 0)


def summed_rows(shard, chips, core, dim):
    sizes = (lax.axis_size(chips), lax.axis_size(core))
    pieces = in_blocks(shard, dim, sizes[0] * sizes[1])
    inside = pieces.shape[1:]
    pieces = pieces.reshape(*sizes, *inside).swapaxes(0, 1).reshape(-1, *inside)
    pieces = lax.psum_scatter(pieces, core, scatter_dimension=0, tiled=True)
    return lax.psum_scatter(pieces, chips, scatter_dimension=0, tiled=True)[0]


def tables(length):
    within = jnp.arange(HD, dtype=jnp.int32) // 2
    rates = jnp.power(jnp.float32(rope_base), within.astype(F32) * (-2.0 / HD))
    angle = jnp.arange(length, dtype=F32)[:, None] * rates[None, :]
    return jnp.cos(angle), jnp.sin(angle)


def rotate(matrix, cos, sin):
    even = jnp.arange(matrix.shape[1]) % 2 == 0
    partner = jnp.where(even[None, :], -jnp.roll(matrix, -1, axis=1), jnp.roll(matrix, 1, axis=1))
    return matrix * cos + partner * sin


def per_device(
    tokens, cotangent, gain, w_query, w_key, w_value, moment_query, moment_key, moment_value
):
    query_width = w_query.shape[1]
    key_width = w_key.shape[1]
    width = tokens.shape[2]
    in_scale = width ** (-0.5)
    w_head = lax.all_gather(jnp.stack([w_key, w_value]), SHARE, axis=2, tiled=True)
    w_all = jnp.concatenate([w_query, w_head[0], w_head[1]], axis=1)
    inputs = tokens[0].astype(F32)
    reciprocal = lax.rsqrt(jnp.mean(inputs * inputs, axis=1, keepdims=True) + norm_eps)
    unit_rows = inputs * reciprocal
    normed = (unit_rows * gain).astype(BF)
    normed_all = lax.all_gather(normed, TENSOR, axis=0, tiled=True)
    length = normed_all.shape[0]
    cos, sin = tables(length)
    cos3, sin3 = jnp.tile(cos, (1, 3)), jnp.tile(sin, (1, 3))
    projected = jnp.dot(normed_all, w_all, preferred_element_type=F32) * in_scale
    turned = rotate(projected[:, : 3 * HD], cos3, sin3).astype(BF)
    values = projected[:, 3 * HD :].astype(BF)
    attended, grad_query, key_part, value_part = attention(
        turned[:, : 2 * HD], turned[:, 2 * HD :], values, cotangent[0], cos, sin
    )
    grads = jnp.concatenate([grad_query, key_part, value_part], axis=1)
    term = jnp.einsum("sc,dc->sd", grads, w_all, preferred_element_type=F32) * in_scale
    grad_normed = summed_rows(term.astype(BF), CHIPS, "core", 0).astype(F32)
    grad_unit = grad_normed * gain
    inner = jnp.mean(grad_unit * unit_rows, axis=1, keepdims=True)
    grad_tokens = (reciprocal * (grad_unit - unit_rows * inner)).astype(BF)[None]
    pair = lax.psum_scatter(
        jnp.stack([key_part, value_part]), SHARE, scatter_dimension=2, tiled=True
    )
    mine = jnp.concatenate([grad_query, pair[0], pair[1]], axis=1)
    grad_w = (
        jnp.einsum("sd,sc->dc", normed_all, mine, preferred_element_type=F32) * in_scale
    ).astype(BF)
    summed = lax.psum_scatter(grad_w, DP, scatter_dimension=0, tiled=True).astype(F32)
    total = lax.psum(jnp.sum(summed * summed), ALL)
    count_all = 1.0 * D * HD * (HEADS + 2 * KVH)
    factor = lax.rsqrt(total / count_all + stat_eps)
    dp_rank = lax.axis_index(DP)
    share = moment_query.shape[0]
    w_mine = jnp.concatenate([w_query, w_key, w_value], axis=1)
    own = lax.dynamic_slice_in_dim(w_mine, dp_rank * share, share, 0).astype(F32)
    moment = jnp.concatenate([moment_query, moment_key, moment_value], axis=1)
    moved = keep_rate * moment + summed * factor
    fresh = lax.all_gather((own - learn_rate * moved).astype(BF), DP, axis=0, tiled=True)
    ends = [query_width, query_width + key_width]
    fresh_query, fresh_key, fresh_value = jnp.split(fresh, ends, axis=1)
    next_query, next_key, next_value = jnp.split(moved, ends, axis=1)
    return (
        attended[None],
        grad_tokens,
        fresh_query,
        fresh_key,
        fresh_value,
        next_query,
        next_key,
        next_value,
    )


def solution(mesh):
    torus = Mesh(mesh.devices.reshape(2, 4, 2, 2, 2, 2), ALL)
    placed = (
        P(DP, TENSOR, None),
        P(DP, None, TENSOR),
        P(),
        P(None, TENSOR),
        P(None, TENSOR),
        P(None, TENSOR),
        P(DP, TENSOR),
        P(DP, TENSOR),
        P(DP, TENSOR),
    )
    return jax.shard_map(
        per_device,
        mesh=torus,
        in_specs=placed,
        out_specs=(
            P(DP, None, TENSOR),
            P(DP, TENSOR, None),
            P(None, TENSOR),
            P(None, TENSOR),
            P(None, TENSOR),
            P(DP, TENSOR),
            P(DP, TENSOR),
            P(DP, TENSOR),
        ),
        check_vma=False,
    )
```

time: 781 us -> 548 us (0.70)
  matrix products: 299 us -> 38.3 us
  waiting for transfers between devices: 258 us -> 318 us
  local copies, waits for them, and re-layouts: 105 us -> 57.5 us
  Pallas kernels: 0 us -> 31 us
  blocking collectives: 36.2 us -> 63.8 us
  other arithmetic: 47.3 us -> 21.2 us
  loops' own time: 8.27 us -> 0 us
    dot_general x29 -> x3, matrix products: 267 us -> 38.3 us  [the longest x1 14.2 us: per_device(): jnp.einsum('sc,dc->sd', grads, w_all, preferred_element_type=F32) * in_scale]
    dynamic_update_slice x12 -> x0, local copies, waits for them, and re-layouts: 49.8 us -> none  [per_device(): lax.scan(attend, (empty, empty), starts)]
    unnamed x5 -> x8, waiting for transfers between devices: 0.57 us -> 38.5 us
    sub x4 -> x0, matrix products: 32 us -> none  [attend(): attention = jax.nn.softmax(jnp.where(causal[None], scores, -1e+30), axis=2)]
    pallas_call x0 -> x1, Pallas kernels: none -> 31 us  [attention(): pl.pallas_call(functools.partial(attn_kernel, BQ, TC, HD ** (-0.5)), grid...]
    psum x5 -> x1, blocking collectives: 36.2 us -> 63.8 us  [per_device(): total = lax.psum(jnp.sum(summed * summed), ALL)]
    convert_element_type x10 -> x4, other arithmetic: 30.7 us -> 9 us  [the longest x1 2.76 us: per_device(): (reciprocal * (grad_unit - unit_rows * inner)).astype(BF)[None]]
    all_gather x1 -> x2, waiting for transfers between devices: 33.9 us -> 46.7 us  [the longest x1 36.4 us: per_device(): lax.all_gather((own - learn_rate * moved).astype(BF), DP, axis=0, tiled=T...]
  transfers between devices with their start and end apart: 9 -> 7, of which waited for: 5 -> 6; matrix products, arithmetic and copies ran while one was open for 17% -> 13% of each run, Pallas kernels for 0% -> 0%
where the time goes in v1:
time: 548 us; the launch traced here: 546 us
  waiting for transfers between devices  318 us (58%)
  blocking collectives  63.8 us (12%)
  local copies, waits for them, and re-layouts  57.5 us (10%)
  matrix products  38.3 us (7%)
  Pallas kernels  31 us (6%)
  other arithmetic  21.2 us (4%)
  between operations  15.7 us (3%)
    reduce_scatter x1, waiting for transfers between devices, summed_rows(): return lax.psum_scatter(pieces, chips, scatter_dimension=0, tiled=True)[0]  112 us
    all_gather x1, waiting for transfers between devices, per_device(): normed_all = lax.all_gather(normed, TENSOR, axis=0, tiled=True)  110 us
    psum x1, blocking collectives, per_device(): total = lax.psum(jnp.sum(summed * summed), ALL)  63.8 us
    unnamed x8, waiting for transfers between devices  38.5 us
    all_gather x1, waiting for transfers between devices, per_device(): lax.all_gather((own - learn_rate * moved).astype(BF), DP, axis=0, tiled=T...  36.4 us
    pallas_call x1, Pallas kernels, attention(): pl.pallas_call(functools.partial(attn_kernel, BQ, TC, HD ** (-0.5)), grid...  31 us
    dot_general x1, matrix products, per_device(): jnp.einsum('sc,dc->sd', grads, w_all, preferred_element_type=F32) * in_scale  14.2 us
    transpose x1, local copies, waits for them, and re-layouts, summed_rows(): pieces = pieces.reshape(*sizes, *inside).swapaxes(0, 1).reshape(-1, *inside)  14.1 us
  transfers between devices with their start and end apart: 7, of which 6 were waited for; matrix products, arithmetic and copies ran while one was open for 13% of the time, Pallas kernels for 0%

profile of v1, /device:TPU:0, one launch (start us, length us, event | category | flops | bytes accessed | tf_op | source)
XLA Modules:
  0.0 546.4 jit_solution(14393289244795524008)
XLA Ops:
  10.8 2.0 fusion.9
  12.9 3.9 fusion.27
  18.4 3.3 tile.8
  21.7 3.7 copy.41
  25.7 2.2 tile.20
  27.8 3.6 copy.43
  31.4 10.2 %all-gather.6.cloned.1.call-done = bf16[2,4096,128]{1,2,0:T(8,128)(2,1)} async-done(((bf16[2,4096,32]{1,2,0:T(8,128)(2,1)}), bf16[2,4096,128]{1,2,0:T(8,128)(2,1)}) %all-gather.6.cloned.1.call-update) | async-done | bytes 2097168 | tf_op jit(solution)/shard_map/all_gather | solution.py:181
  45.3 109.6 %all-gather.4.cloned.1.call-done = bf16[2048,4096]{1,0:T(8,128)(2,1)} async-done(((bf16[128,4096]{1,0:T(8,128)(2,1)}), bf16[2048,4096]{1,0:T(8,128)(2,1)}) %all-gather.4.cloned.1.call-update) | async-done | bytes 16777232 | tf_op jit(solution)/shard_map/all_gather | solution.py:187
  154.9 12.9 %convolution_multiply_fusion.1 = f32[2048,512]{1,0:T(8,128)S(1)} fusion(bf16[2048,4096]{1,0:T(8,128)(2,1)} %all-gather.4.cloned.1.call-done, bf16[4096,128]{1,0:T(8,128)(2,1)S(1)} %copy.38, bf16[4096,128]{1,0:T(8,128)(2,1)} %copy.37, bf16[4096,256]{1,0:T(8,128)(2,1)} %param.12), kind=kOutput, calls=%fused_computation.4 | convolution fusion | flops 8603566080 | bytes 25165824 | tf_op jit(solution)/shard_map/dot_general | solution.py:191
  175.8 31.0 %attention.1 = (bf16[2048,256]{1,0:T(8,128)(2,1)}, bf16[2048,256]{1,0:T(8,128)(2,1)}, bf16[2048,128]{1,0:T(8,128)(2,1)}, bf16[2048,128]{1,0:T(8,128)(2,1)}) custom-call(bf16[2048,256]{1,0:T(8,128)(2,1)} %slice.64.q_ref, bf16[2048,128]{1,0:T(8,128)(2,1)} %slice.65.k_ref, bf16[2048,128]{1,0:T(8,128)(2,1)} %slice.75.v_ref, bf16[2048,256]{1,0:T(8,128)(2,1)} %bitcast.47, ...), custom_call_target="tpu_custom_call" | custom-call | tf_op jit(solution)/shard_map/attention/pallas_call | solution.py:132
  208.1 2.0 copy.47
  211.6 37.8 %all-reduce.3.cloned.1.call-done = bf16[2,2048,128]{1,0,2:T(2,128)(2,1)} async-done(((bf16[2,2048,128]{1,0,2:T(2,128)(2,1)}), bf16[2,2048,128]{1,0,2:T(2,128)(2,1)}) %all-reduce.3.cloned.1.call-update) | async-done | bytes 1048592
  253.0 11.2 %fusion = bf16[4096,320]{0,1:T(8,128)(2,1)} fusion(bf16[2048,4096]{1,0:T(8,128)(2,1)} %all-gather.4.cloned.1.call-done, bf16[2048,32]{1,0:T(8,128)(2,1)} %bitcast.51, bf16[2048,32]{1,0:T(8,128)(2,1)} %bitcast.50, bf16[2048,256]{1,0:T(8,128)(2,1)} %get-tuple-element.13), kind=kOutput, calls=%fused_computation.2 | convolution fusion | flops 5375262720 | bytes 20709376 | tf_op jit(solution)/shard_map/sd,sc->dc/dot_general | solution.py:208
  264.3 14.2 %multiply_convert_fusion = bf16[2048,4096]{1,0:T(8,128)(2,1)} fusion(bf16[2048,128]{1,0:T(8,128)(2,1)} %get-tuple-element.15, bf16[2048,128]{1,0:T(8,128)(2,1)} %get-tuple-element.14, bf16[2048,256]{1,0:T(8,128)(2,1)} %get-tuple-element.13, bf16[4096,128]{1,0:T(8,128)(2,1)} %copy-done.7, bf16[4096,128]{1,0:T(8,128)(2,1)} %copy.37, ...), kind=kOutput, calls=%fused_computation | convolution fusion | flops 8625586176 | bytes 23068672 | tf_op jit(solution)/shard_map/sc,dc->sd/dot_general | solution.py:198
  278.5 14.1 %copy.44 = bf16[2,8,128,4096]{3,2,1,0:T(8,128)(2,1)} copy(bf16[2,8,128,4096]{3,2,0,1:T(8,128)(2,1)} %bitcast.44) | data formatting | bytes 33554432 | tf_op jit(solution)/shard_map/transpose | solution.py:156
  292.7 3.0 copy.45
  295.7 2.0 copy.46
  297.7 12.0 %reduce-scatter.8.cloned.1.call-done = bf16[512,320]{0,1:T(8,128)(2,1)} async-done(((bf16[4096,320]{0,1:T(8,128)(2,1)}), bf16[512,320]{0,1:T(8,128)(2,1)}) %reduce-scatter.8.cloned.1.call-update) | async-done | bytes 327696 | tf_op jit(solution)/shard_map/reduce_scatter | solution.py:210
  311.4 63.8 %psum.7 = f32[]{:T(128)} all-reduce(f32[]{:T(128)} %fusion.29), channel_id=1, replica_groups=mesh['dp_0'=2,'dp_1'=4,'x'=2,'yh'=2,'yl'=2,'core'=2] {'dp_0','dp_1','x',..., use_global_device_ids=true, to_apply=%region_7.8 | all-reduce | flops 1 | bytes 8 | tf_op jit(solution)/shard_map/psum | solution.py:211
  376.0 2.3 subtract_convert_fusion
  381.2 36.4 %all-gather.8.cloned.1.call-done = bf16[4096,320]{0,1:T(8,128)(2,1)} async-done(((bf16[512,320]{0,1:T(8,128)(2,1)}), bf16[4096,320]{0,1:T(8,128)(2,1)}) %all-gather.8.cloned.1.call-update) | async-done | bytes 2621456 | tf_op jit(solution)/shard_map/all_gather | solution.py:220
  419.2 2.4 copy.50
  423.5 111.5 %reduce-scatter.6.cloned.1.call-done = bf16[1,128,4096]{2,1,0:T(8,128)(2,1)} async-done(((bf16[8,128,4096]{2,1,0:T(8,128)(2,1)}), bf16[1,128,4096]{2,1,0:T(8,128)(2,1)}) %reduce-scatter.6.cloned.1.call-update) | async-done | bytes 1048592 | tf_op jit(solution)/shard_map/reduce_scatter | solution.py:158
  536.8 2.8 fusion.13
  (71 shorter events, 32.8 us)
Async XLA Ops:
  7.2 3.6 copy-start
  7.2 34.5 %all-gather.6.cloned.1.call-start = ((), (), s32[]{:S(2)}) async-start(), calls=%async_computation.4 | async-start | bytes 2621440 | tf_op jit(solution)/shard_map/all_gather | solution.py:181
  9.2 145.7 %all-gather.4.cloned.1.call-start = ((), (), s32[]{:S(2)}) async-start(), calls=%async_computation.3 | async-start | bytes 17825792 | tf_op jit(solution)/shard_map/all_gather | solution.py:187
  12.8 236.6 %all-reduce.3.cloned.1.call-start = ((), (), s32[]{:S(2)}) async-start(), calls=%async_computation.9 | async-start | bytes 2097152
  16.8 4.9 copy-start.4
  16.8 8.6 %copy-start.3 = (f32[2048,128]{1,0:T(8,128)}, f32[2048,128]{1,0:T(8,128)S(1)}, u32[]{:S(2)}) copy-start(f32[2048,128]{1,0:T(8,128)S(1)} %get-tuple-element.54.sin_ref) | copy-start | bytes 3145732
  45.3 122.5 %copy-start.7 = (bf16[4096,128]{1,0:T(8,128)(2,1)}, bf16[4096,128]{1,0:T(8,128)(2,1)S(1)}, u32[]{:S(2)}) copy-start(bf16[4096,128]{1,0:T(8,128)(2,1)S(1)} %copy.38) | copy-start | bytes 3145732
  167.8 1.9 copy-start.2
  168.9 2.1 copy-start.1
  206.8 3.6 copy-start.12
  210.1 99.6 %reduce-scatter.8.cloned.1.call-start = ((), (), s32[]{:S(2)}) async-start(), calls=%async_computation.7 | async-start | bytes 2949120 | tf_op jit(solution)/shard_map/reduce_scatter | solution.py:210
  253.0 11.3 %copy-start.6 = (bf16[4096,256]{1,0:T(8,128)(2,1)S(1)}, bf16[4096,256]{1,0:T(8,128)(2,1)}, u32[]{:S(2)}) copy-start(bf16[4096,256]{1,0:T(8,128)(2,1)} %param.12) | copy-start | bytes 6291460
  264.2 114.2 %reduce-scatter.4.cloned.1.call-start = ((), (), s32[]{:S(2)}) async-start(), calls=%async_computation.5 | async-start | bytes 25165824 | tf_op jit(solution)/shard_map/reduce_scatter | solution.py:157
  292.6 83.4 %copy-start.8 = (bf16[4096,32]{0,1:T(8,128)(2,1)S(1)}, bf16[4096,32]{0,1:T(8,128)(2,1)}, u32[]{:S(2)}) copy-start(bf16[4096,32]{0,1:T(8,128)(2,1)} %param.14) | copy-start | bytes 786436
  292.6 83.4 %copy-start.10 = (f32[512,32]{0,1:T(8,128)S(1)}, f32[512,32]{0,1:T(8,128)}, u32[]{:S(2)}) copy-start(f32[512,32]{0,1:T(8,128)} %param.17) | copy-start | bytes 196612
  292.6 83.4 %copy-start.11 = (f32[512,32]{0,1:T(8,128)S(1)}, f32[512,32]{0,1:T(8,128)}, u32[]{:S(2)}) copy-start(f32[512,32]{0,1:T(8,128)} %param.16) | copy-start | bytes 196612
  292.6 125.0 %all-gather.8.cloned.1.call-start = ((), (), s32[]{:S(2)}) async-start(), calls=%async_computation.8 | async-start | bytes 2949120 | tf_op jit(solution)/shard_map/all_gather | solution.py:220
  378.3 156.7 %reduce-scatter.6.cloned.1.call-start = ((), (), s32[]{:S(2)}) async-start(), calls=%async_computation.6 | async-start | bytes 9437184 | tf_op jit(solution)/shard_map/reduce_scatter | solution.py:158
  378.4 1.1 copy-start.5
  417.6 1.6 slice-start
  419.2 115.8 %copy-start.9 = (f32[4096]{0:T(1024)S(1)}, f32[4096]{0:T(1024)}, u32[]{:S(2)}) copy-start(f32[4096]{0:T(1024)} %param.11) | copy-start | bytes 49156
Sparse Core Ops, SparseCore 0:
  10.3 31.3 all-gather.5
  44.7 110.1 all-gather.3
  210.2 39.1 all-reduce.2
  264.3 45.3 reduce-scatter.7
  312.1 28.2 reduce-scatter.3
  378.4 39.1 all-gather.7
  421.4 113.5 reduce-scatter.5

commit v2 on v1

--- a/solution.py
+++ b/solution.py
@@ -40,7 +40,7 @@
     return lax.dot_general(a,b,dims,preferred_element_type=F32)
 
 def attn_kernel(BQ, TC, hs, q_ref, k_ref, v_ref, do_ref, cos_ref, sin_ref,
-                out_ref, gq_ref, gk_ref, gv_ref, va, s_scr, r_scr, p_scr, dk, dv, m_scr, o_scr, g_scr):
+                out_ref, gq_ref, gkv_ref, va, s_scr, r_scr, p_scr, dk, dv, m_scr, o_scr, g_scr):
     i = pl.program_id(0)
     n = pl.num_programs(0)
     T = k_ref.shape[0]
@@ -121,8 +121,8 @@
     gq_ref[:, HD:] = rope(gq[BQ:], cos, sin, -1.0).astype(BF)
     @pl.when(i == n-1)
     def _():
-        gk_ref[...] = rope(dk[...], cos_ref[...], sin_ref[...], -1.0).astype(BF)
-        gv_ref[...] = dv[...].astype(BF)
+        gkv_ref[:, :HD] = rope(dk[...], cos_ref[...], sin_ref[...], -1.0).astype(BF)
+        gkv_ref[:, HD:] = dv[...].astype(BF)
 
 def attention(q, k, v, do, cos, sin, BQ=512, TC=512):
     T = q.shape[0]
@@ -133,8 +133,8 @@
         functools.partial(attn_kernel, BQ, TC, HD**-0.5),
         grid=(T//BQ,),
         in_specs=[rows, whole, whole, rows, whole, whole],
-        out_specs=[rows, rows, whole, whole],
-        out_shape=[jax.ShapeDtypeStruct((T, 2*HD), BF)]*2 + [jax.ShapeDtypeStruct((T, HD), BF)]*2,
+        out_specs=[rows, rows, pl.BlockSpec((T, 2*HD), lambda i: (0, 0))],
+        out_shape=[jax.ShapeDtypeStruct((T, 2*HD), BF)]*3,
         scratch_shapes=[pltpu.VMEM((T, 2*HD), BF), pltpu.VMEM((T//TC, R, TC), F32), pltpu.VMEM((T//TC, R, TC), F32),
             pltpu.VMEM((T//TC, R, TC), BF), pltpu.VMEM((T, HD), F32), pltpu.VMEM((T, HD), F32),
             pltpu.VMEM((R, HD), F32), pltpu.VMEM((R, 2*HD), F32), pltpu.VMEM((R, HD), F32)],
@@ -143,19 +143,413 @@
     )(q, k, v, do, cos, sin)
 
 
-def in_blocks(shard, dim, size):
-    lengths = shard.shape
-    pieces = shard.reshape(*lengths[:dim], size, lengths[dim] // size, *lengths[dim + 1 :])
-    return jnp.moveaxis(pieces, dim, 0)
-
-
-def summed_rows(shard, chips, core, dim):
-    sizes = (lax.axis_size(chips), lax.axis_size(core))
-    pieces = in_blocks(shard, dim, sizes[0] * sizes[1])
-    inside = pieces.shape[1:]
-    pieces = pieces.reshape(*sizes, *inside).swapaxes(0, 1).reshape(-1, *inside)
-    pieces = lax.psum_scatter(pieces, core, scatter_dimension=0, tiled=True)
-    return lax.psum_scatter(pieces, chips, scatter_dimension=0, tiled=True)[0]
+MESH_ID = pl.DeviceIdType.MESH
+INNER = 4
+
+
+def place():
+    at = lax.axis_index
+    return dict(
+        xl=at("dp_0"), z=at("dp_1"), xh=at("x"), y=at("yh") * 2 + at("yl"), core=at("core")
+    )
+
+
+def device(**moved):
+    names = {}
+    for key, value in moved.items():
+        if key == "y":
+            names["yh"] = value // 2
+            names["yl"] = value % 2
+        elif key == "x":
+            names["x"] = value // 2
+            names["dp_0"] = value % 2
+        else:
+            names[{"xl": "dp_0", "z": "dp_1", "xh": "x", "core": "core"}[key]] = value
+    return names
+
+
+class Link:
+    def __init__(self, send, recv):
+        self.send, self.recv, self.used, self.sent = send, recv, 0, []
+
+    def slot(self):
+        self.used += 1
+        return self.used - 1
+
+    def start(self, slot, src, dst, to):
+        copy = pltpu.make_async_remote_copy(
+            src_ref=src,
+            dst_ref=dst,
+            send_sem=self.send.at[slot],
+            recv_sem=self.recv.at[slot],
+            device_id=to,
+            device_id_type=MESH_ID,
+        )
+        copy.start()
+        self.sent.append(copy)
+
+    def wait(self, slot, landed, to):
+        pltpu.make_async_remote_copy(
+            src_ref=landed,
+            dst_ref=landed,
+            send_sem=self.send.at[slot],
+            recv_sem=self.recv.at[slot],
+            device_id=to,
+            device_id_type=MESH_ID,
+        ).wait_recv()
+
+    def drain(self):
+        for copy in self.sent:
+            copy.wait_send()
+
+
+def added(ref, other):
+    ref[...] = (ref[...].astype(F32) + other[...].astype(F32)).astype(BF)
+
+
+def ring_reduce(link, me, up, down, piece, half, part_low, part_high, full_low, full_high):
+    s = [link.slot() for _ in range(4)]
+    far = piece(lax.rem(me + 2, 4))
+    link.start(s[0], half(far, 0), part_low, up)
+    link.start(s[1], half(far, 1), part_high, down)
+    yield
+    above = piece(lax.rem(me + 1, 4))
+    link.wait(s[0], part_low, down)
+    added(half(above, 0), part_low)
+    link.start(s[2], above, full_low, up)
+    below = piece(lax.rem(me + 3, 4))
+    link.wait(s[1], part_high, up)
+    added(half(below, 1), part_high)
+    link.start(s[3], below, full_high, down)
+    yield
+    link.wait(s[2], full_low, down)
+    link.wait(s[3], full_high, up)
+
+
+def ring_spread(link, me, up, down, piece, half):
+    s = [link.slot() for _ in range(4)]
+    mine = piece(me)
+    link.start(s[0], mine, mine, up)
+    link.start(s[1], mine, mine, down)
+    yield
+    low, high = piece(lax.rem(me + 3, 4)), piece(lax.rem(me + 1, 4))
+    link.wait(s[0], low, down)
+    link.start(s[2], half(low, 0), half(low, 0), up)
+    link.wait(s[1], high, up)
+    link.start(s[3], half(high, 1), half(high, 1), down)
+    yield
+    far = piece(lax.rem(me + 2, 4))
+    link.wait(s[2], half(far, 0), down)
+    link.wait(s[3], half(far, 1), up)
+
+
+def finish(steps):
+    for _ in steps:
+        pass
+
+
+def greet(others):
+    barrier = pltpu.get_barrier_semaphore()
+    for other in others:
+        pl.semaphore_signal(barrier, inc=1, device_id=other, device_id_type=MESH_ID)
+    pl.semaphore_wait(barrier, len(others))
+
+
+def rows_part(first, count):
+    return lambda ref, part: ref.at[pl.ds(first if part == 0 else first + count[0], count[part])]
+
+
+LOW = 64
+
+
+def rows_chain(r, link, p):
+    core, y, xh = p["core"], p["y"], p["xh"]
+    sib, across = device(core=1 - core), device(xh=1 - xh)
+    up, down = device(y=lax.rem(y + 1, 4)), device(y=lax.rem(y + 3, 4))
+    near = y + 1 - 2 * lax.rem(y, 2)
+    pair = device(y=near)
+    gq, gkv, sib_q, sib_kv, cat = r["gq"], r["gkv"], r["sib_q"], r["sib_kv"], r["cat"]
+    one, two = link.slot(), link.slot()
+    link.start(one, gkv.at[:, 1 - core], sib_kv, sib)
+    link.start(two, gq.at[:, 1 - core], sib_q, sib)
+    yield
+    link.wait(one, sib_kv, sib)
+    added(sib_kv, gkv.at[:, core])
+    three = link.slot()
+    link.start(three, sib_kv, r["pair_kv"], pair)
+    link.wait(two, sib_q, sib)
+    cat[:, :, : 2 * HD] = gq[:, core]
+    cat[:, :, 2 * HD : 4 * HD] = sib_q[...]
+    cat[:, :, 4 * HD :] = sib_kv[...]
+    rows = 4 * cat.shape[1]
+    width = r["part"].shape[3]
+    step = 512
+    scale = width ** (-0.5)
+
+    def products(side):
+        left = cat[pl.ds(side * 4, 4)].reshape(rows, 6 * HD)
+
+        def body(c, _):
+            at = pl.ds(pl.multiple_of(c * step, step), step)
+            out = dotg(left, r["w3"][at, :], NT) * scale
+            r["part"][side, :, :, at] = out.astype(BF).reshape(4, rows // 4, step)
+            return 0
+
+        lax.fori_loop(0, width // step, body, 0)
+
+    part = r["part"]
+    high = part.shape[2] - LOW
+    top, rest = pl.ds(0, LOW), pl.ds(LOW, high)
+    cut = lambda n: (lambda ref, i: ref.at[pl.ds(0 if i == 0 else n // 2, n // 2)])
+
+    def ring(side, rows_at, n, bufs):
+        return ring_reduce(
+            link, y, up, down, lambda q: part.at[side, q, rows_at], cut(n), *bufs
+        )
+
+    def bufs(k):
+        return tuple(r[name].at[k] for name in ("part_low", "part_high", "full_low", "full_high"))
+
+    products(1 - xh)
+    across_slots = [link.slot() for _ in range(4)]
+    for q in range(4):
+        link.start(across_slots[q], part.at[1 - xh, q, rest], r["cross"].at[q], across)
+    far_ring = ring(1 - xh, top, LOW, bufs(0))
+    next(far_ring)
+    products(xh)
+    near_ring = ring(xh, top, LOW, bufs(1))
+    next(near_ring)
+    yield
+    link.wait(three, r["pair_kv"], pair)
+    total = (sib_kv[...].astype(F32) + r["pair_kv"][...].astype(F32)).astype(BF)
+    r["kv_all"][:, core] = total
+    four = link.slot()
+    link.start(four, r["kv_all"].at[:, core], r["kv_all"].at[:, core], sib)
+    next(far_ring)
+    link.wait(four, r["kv_all"].at[:, 1 - core], sib)
+    yield
+    next(near_ring)
+    yield
+    finish(far_ring)
+    k = 0
+    done = part.at[1 - xh, y, top]
+    done[...] = (
+        done[...].astype(F32)
+        + r["full_low"][k].astype(F32)
+        + r["full_high"][k].astype(F32)
+    ).astype(BF)
+    last = link.slot()
+    link.start(last, done, r["cross_top"], across)
+    yield
+    for q in range(4):
+        link.wait(across_slots[q], r["cross"].at[q], across)
+        added(part.at[xh, q, rest], r["cross"].at[q])
+    rest_ring = ring(xh, rest, high, bufs(2))
+    next(rest_ring)
+    yield
+    finish(near_ring)
+    next(rest_ring)
+    yield
+    finish(rest_ring)
+    link.wait(last, r["cross_top"], across)
+    own = part.at[xh, y]
+    top_rows = (
+        own[top].astype(F32)
+        + r["full_low"][1].astype(F32)
+        + r["full_high"][1].astype(F32)
+        + r["cross_top"][...].astype(F32)
+    )
+    rest_rows = (
+        own[rest].astype(F32) + r["full_low"][2].astype(F32) + r["full_high"][2].astype(F32)
+    )
+    for first, grad_normed in ((0, top_rows), (LOW, rest_rows)):
+        at = pl.ds(first, grad_normed.shape[0])
+        inputs = r["tokens"][at, :].astype(F32)
+        reciprocal = lax.rsqrt(jnp.mean(inputs * inputs, axis=1, keepdims=True) + norm_eps)
+        unit = inputs * reciprocal
+        grad_unit = grad_normed * r["gain"][...]
+        inner = jnp.mean(grad_unit * unit, axis=1, keepdims=True)
+        r["grad_tokens"][at, :] = (reciprocal * (grad_unit - unit * inner)).astype(BF)
+
+
+def weight_chain(r, link, p):
+    core, y, xh, xl, z = p["core"], p["y"], p["xh"], p["xl"], p["z"]
+    up, down = device(z=lax.rem(z + 1, 4)), device(z=lax.rem(z + 3, 4))
+    beside = device(xl=1 - xl)
+    wide = 2 * HD
+    thin = HD // INNER
+    length = r["turned"].shape[1]
+    width = r["rows"].shape[0] * r["rows"].shape[2]
+    scale = width ** (-0.5)
+    which = pl.multiple_of((lax.rem(y, 2) * 2 + core) * thin, thin)
+    r["turned"][:wide, :] = r["gq"][...].reshape(length, wide).T
+    r["kv_turned"][...] = r["kv_all"][...].reshape(length, wide).T
+    r["turned"][wide : wide + thin, :] = r["kv_turned"][pl.ds(which, thin), :]
+    r["turned"][wide + thin :, :] = r["kv_turned"][pl.ds(which + HD, thin), :]
+    grad = r["grad"]
+
+    def body(c, _):
+        r["arrive"](c)
+        out = jnp.dot(r["turned"][...], r["rows"][c], preferred_element_type=F32) * scale
+        grad[c % 4, c // 4] = out.astype(BF)
+        return 0
+
+    lax.fori_loop(0, 8, body, 0)
+    index = lambda ref, i: ref.at[i]
+    ring = ring_reduce(
+        link, z, up, down, lambda q: grad.at[q], index, r["z_low"], r["z_high"], r["z_full_low"], r["z_full_high"]
+    )
+    next(ring)
+    yield
+    next(ring)
+    yield
+    finish(ring)
+    mine = grad.at[z]
+    mine[...] = (
+        mine[...].astype(F32) + r["z_full_low"][...].astype(F32) + r["z_full_high"][...].astype(F32)
+    ).astype(BF)
+    s = link.slot()
+    link.start(s, mine.at[1 - xl], r["beside"], beside)
+    yield
+    link.wait(s, r["beside"], beside)
+    summed = mine[xl].astype(F32) + r["beside"][...].astype(F32)
+    r["summed"][...] = summed
+    square = jnp.sum(summed * summed, axis=0, keepdims=True)
+    square = jnp.sum(square, axis=1, keepdims=True)
+    x = xh * 2 + xl
+    stages = (
+        [device(core=1 - core)],
+        [device(x=lax.rem(x + i, 4)) for i in (1, 2, 3)],
+        [device(y=lax.rem(y + i, 4)) for i in (1, 2, 3)],
+        [device(z=lax.rem(z + i, 4)) for i in (1, 2, 3)],
+    )
+    total = jnp.broadcast_to(square, (8, HD))
+    for k, others in enumerate(stages):
+        r["square"][k] = total
+        slots = [link.slot() for _ in others]
+        for i, other in enumerate(others):
+            link.start(slots[i], r["square"].at[k], r["squares"].at[k, i], other)
+        yield
+        for i, other in enumerate(others):
+            back = others[len(others) - 1 - i]
+            link.wait(slots[i], r["squares"].at[k, i], back)
+            total = total + r["squares"][k, i]
+    count_all = 1.0 * D * HD * (HEADS + 2 * KVH)
+    factor = lax.rsqrt(total[:1, :1] / count_all + stat_eps)
+    moved = keep_rate * r["moment"][...] + r["summed"][...] * factor
+    r["next"][...] = moved
+    fresh = r["fresh"]
+    fresh[z, xl] = (r["own"][...].astype(F32) - learn_rate * moved).astype(BF)
+    s = link.slot()
+    link.start(s, fresh.at[z, xl], fresh.at[z, xl], beside)
+    n = r["own"].shape[0] // 2
+    cut = lambda ref, i: ref.at[pl.ds(i * n, n)]
+    first = ring_spread(link, z, up, down, lambda q: fresh.at[q, xl], cut)
+    next(first)
+    yield
+    link.wait(s, fresh.at[z, 1 - xl], beside)
+    second = ring_spread(link, z, up, down, lambda q: fresh.at[q, 1 - xl], cut)
+    next(second)
+    next(first)
+    yield
+    finish(first)
+    next(second)
+    yield
+    finish(second)
+
+
+ROW_NAMES = ("gq", "gkv", "w3", "tokens", "gain", "rows_hbm", "moment", "own")
+OUT_NAMES = ("grad_tokens", "fresh", "next")
+
+
+def back_kernel(names, *refs):
+    r = dict(zip(names, refs))
+    p = place()
+    link = Link(r["send"], r["recv"])
+    copies = []
+    step = r["rows"].shape[2]
+    for c in range(8):
+        copy = pltpu.make_async_copy(
+            r["rows_hbm"].at[:, pl.ds(c * step, step)], r["rows"].at[c], r["load"].at[c]
+        )
+        copy.start()
+
+    def arrive(c):
+        pltpu.make_async_copy(
+            r["rows_hbm"].at[:, pl.ds(pl.multiple_of(c * step, step), step)], r["rows"].at[c], r["load"].at[c]
+        ).wait()
+
+    r["arrive"] = arrive
+    x = p["xh"] * 2 + p["xl"]
+    others = [device(core=1 - p["core"])]
+    for i in (1, 2, 3):
+        others.append(device(x=lax.rem(x + i, 4)))
+        others.append(device(y=lax.rem(p["y"] + i, 4)))
+        others.append(device(z=lax.rem(p["z"] + i, 4)))
+    greet(others)
+    rows, weights = rows_chain(r, link, p), weight_chain(r, link, p)
+    for which in ORDER:
+        next(rows if which == "r" else weights, None)
+    finish(rows)
+    finish(weights)
+    link.drain()
+
+
+ORDER = "rrrr" + "wrwrwrwrwrw"
+
+
+def back(gq, gkv, w3, tokens, gain, rows, moment, own):
+    length, width = rows.shape
+    columns, share = own.shape
+    block = length // 16
+    halves = (block - LOW, LOW)
+    v = pltpu.VMEM
+    scratch = dict(
+        sib_q=v((8, block, 2 * HD), BF),
+        sib_kv=v((8, block, 2 * HD), BF),
+        pair_kv=v((8, block, 2 * HD), BF),
+        kv_all=v((8, 2, block, 2 * HD), BF),
+        cat=v((8, block, 6 * HD), BF),
+        part=v((2, 4, block, width), BF),
+        part_low=v((3, LOW // 2, width), BF),
+        part_high=v((3, LOW // 2, width), BF),
+        full_low=v((3, LOW, width), BF),
+        full_high=v((3, LOW, width), BF),
+        cross=v((4, block - LOW, width), BF),
+        cross_top=v((LOW, width), BF),
+        rows=v((8, length, width // 8), BF),
+        load=pltpu.SemaphoreType.DMA((8,)),
+        turned=v((columns, length), BF),
+        kv_turned=v((2 * HD, length), BF),
+        grad=v((4, 2, columns, share), BF),
+        z_low=v((columns, share), BF),
+        z_high=v((columns, share), BF),
+        z_full_low=v((2, columns, share), BF),
+        z_full_high=v((2, columns, share), BF),
+        beside=v((columns, share), BF),
+        summed=v((columns, share), F32),
+        square=v((4, 8, HD), F32),
+        squares=v((4, 3, 8, HD), F32),
+        send=pltpu.SemaphoreType.DMA((48,)),
+        recv=pltpu.SemaphoreType.DMA((48,)),
+    )
+    whole = pl.BlockSpec(memory_space=pltpu.VMEM)
+    names = ROW_NAMES + OUT_NAMES + tuple(scratch)
+    return pl.pallas_call(
+        functools.partial(back_kernel, names),
+        in_specs=[pl.BlockSpec(memory_space=pl.ANY) if n == "rows_hbm" else whole for n in ROW_NAMES],
+        out_specs=[whole] * 3,
+        out_shape=[
+            jax.ShapeDtypeStruct((block, width), BF),
+            jax.ShapeDtypeStruct((4, 2, columns, share), BF),
+            jax.ShapeDtypeStruct((columns, share), F32),
+        ],
+        scratch_shapes=list(scratch.values()),
+        compiler_params=pltpu.CompilerParams(
+            collective_id=1, has_side_effects=True, vmem_limit_bytes=62 * 1024 * 1024
+        ),
+        name="back",
+    )(gq, gkv, w3, tokens, gain, rows, moment, own)
 
 
 def tables(length):
@@ -179,6 +573,8 @@
     width = tokens.shape[2]
     in_scale = width ** (-0.5)
     w_head = lax.all_gather(jnp.stack([w_key, w_value]), SHARE, axis=2, tiled=True)
+    w_other = lax.ppermute(w_query, "core", [(0, 1), (1, 0)])
+    w3 = jnp.concatenate([w_query, w_other, w_head[0], w_head[1]], axis=1)
     w_all = jnp.concatenate([w_query, w_head[0], w_head[1]], axis=1)
     inputs = tokens[0].astype(F32)
     reciprocal = lax.rsqrt(jnp.mean(inputs * inputs, axis=1, keepdims=True) + norm_eps)
@@ -191,39 +587,33 @@
     projected = jnp.dot(normed_all, w_all, preferred_element_type=F32) * in_scale
     turned = rotate(projected[:, : 3 * HD], cos3, sin3).astype(BF)
     values = projected[:, 3 * HD :].astype(BF)
-    attended, grad_query, key_part, value_part = attention(
+    attended, grad_query, grad_kv = attention(
         turned[:, : 2 * HD], turned[:, 2 * HD :], values, cotangent[0], cos, sin
     )
-    grads = jnp.concatenate([grad_query, key_part, value_part], axis=1)
-    term = jnp.einsum("sc,dc->sd", grads, w_all, preferred_element_type=F32) * in_scale
-    grad_normed = summed_rows(term.astype(BF), CHIPS, "core", 0).astype(F32)
-    grad_unit = grad_normed * gain
-    inner = jnp.mean(grad_unit * unit_rows, axis=1, keepdims=True)
-    grad_tokens = (reciprocal * (grad_unit - unit_rows * inner)).astype(BF)[None]
-    pair = lax.psum_scatter(
-        jnp.stack([key_part, value_part]), SHARE, scatter_dimension=2, tiled=True
-    )
-    mine = jnp.concatenate([grad_query, pair[0], pair[1]], axis=1)
-    grad_w = (
-        jnp.einsum("sd,sc->dc", normed_all, mine, preferred_element_type=F32) * in_scale
-    ).astype(BF)
-    summed = lax.psum_scatter(grad_w, DP, scatter_dimension=0, tiled=True).astype(F32)
-    total = lax.psum(jnp.sum(summed * summed), ALL)
-    count_all = 1.0 * D * HD * (HEADS + 2 * KVH)
-    factor = lax.rsqrt(total / count_all + stat_eps)
     dp_rank = lax.axis_index(DP)
     share = moment_query.shape[0]
     w_mine = jnp.concatenate([w_query, w_key, w_value], axis=1)
-    own = lax.dynamic_slice_in_dim(w_mine, dp_rank * share, share, 0).astype(F32)
-    moment = jnp.concatenate([moment_query, moment_key, moment_value], axis=1)
-    moved = keep_rate * moment + summed * factor
-    fresh = lax.all_gather((own - learn_rate * moved).astype(BF), DP, axis=0, tiled=True)
+    own = lax.dynamic_slice_in_dim(w_mine, dp_rank * share, share, 0).T
+    moment = jnp.concatenate([moment_query, moment_key, moment_value], axis=1).T
+    by_block = (8, 2, length // 16, 2 * HD)
+    grad_tokens, fresh, moved = back(
+        grad_query.reshape(by_block),
+        grad_kv.reshape(by_block),
+        w3,
+        tokens[0],
+        gain[None],
+        normed_all,
+        moment,
+        own,
+    )
+    moved = moved.T
+    fresh = fresh.transpose(1, 0, 3, 2).reshape(width, -1)
     ends = [query_width, query_width + key_width]
     fresh_query, fresh_key, fresh_value = jnp.split(fresh, ends, axis=1)
     next_query, next_key, next_value = jnp.split(moved, ends, axis=1)
     return (
         attended[None],
-        grad_tokens,
+        grad_tokens[None],
         fresh_query,
         fresh_key,
         fresh_value,

time: 548 us -> 353 us (0.64)
  waiting for transfers between devices: 318 us -> 94.9 us
  Pallas kernels: 31 us -> 152 us
  blocking collectives: 63.8 us -> 0 us
  matrix products: 38.3 us -> 12.6 us
    reduce_scatter x3 -> x0, waiting for transfers between devices: 124 us -> none  [the longest x1 112 us: summed_rows(): return lax.psum_scatter(pieces, chips, scatter_dimension=0, tiled=True)[0]]
    pallas_call x0 -> x1, Pallas kernels: none -> 121 us  [back(): pl.pallas_call(functools.partial(back_kernel, names), in_specs=[pl.BlockS...]
    psum x1 -> x0, blocking collectives: 63.8 us -> none  [per_device(): total = lax.psum(jnp.sum(summed * summed), ALL)]
    unnamed x8 -> x2, waiting for transfers between devices: 38.5 us -> 0.03 us
    all_gather x1 -> x0, waiting for transfers between devices: 36.4 us -> none  [per_device(): lax.all_gather((own - learn_rate * moved).astype(BF), DP, axis=0, tiled=T...]
    dot_general x2 -> x0, matrix products: 25.4 us -> none  [the longest x1 14.2 us: per_device(): jnp.einsum('sc,dc->sd', grads, w_all, preferred_element_type=F32) * in_scale]
    all_gather x1, waiting for transfers between devices: 110 us -> 90.6 us  [per_device(): normed_all = lax.all_gather(normed, TENSOR, axis=0, tiled=True)]
    unnamed x33 -> x29, local copies, waits for them, and re-layouts: 13.3 us -> 22.8 us
  transfers between devices with their start and end apart: 7 -> 3, of which waited for: 6 -> 2; matrix products, arithmetic and copies ran while one was open for 13% -> 14% of each run, Pallas kernels for 0% -> 0%
where the time goes in v2:
time: 353 us
  Pallas kernels  152 us (43%)
  waiting for transfers between devices  94.9 us (27%)
  local copies, waits for them, and re-layouts  60.4 us (17%)
  other arithmetic  17.9 us (5%)
  between operations  14.2 us (4%)
  matrix products  12.6 us (4%)
    pallas_call x1, Pallas kernels, back(): pl.pallas_call(functools.partial(back_kernel, names), in_specs=[pl.BlockS...  121 us
    all_gather x1, waiting for transfers between devices, per_device(): normed_all = lax.all_gather(normed, TENSOR, axis=0, tiled=True)  90.6 us
    pallas_call x1, Pallas kernels, attention(): pl.pallas_call(functools.partial(attn_kernel, BQ, TC, HD ** (-0.5)), grid...  31 us
    unnamed x29, local copies, waits for them, and re-layouts  22.8 us
    dot_general x1, matrix products, per_device(): jnp.dot(normed_all, w_all, preferred_element_type=F32) * in_scale  12.6 us
    another operation x4, local copies, waits for them, and re-layouts, per_device(): cos3, sin3 = (jnp.tile(cos, (1, 3)), jnp.tile(sin, (1, 3)))  8.23 us
    slice x1, local copies, waits for them, and re-layouts, per_device(): w_all = jnp.concatenate([w_query, w_head[0], w_head[1]], axis=1)  7.44 us
  transfers between devices with their start and end apart: 3, of which 2 were waited for; matrix products, arithmetic and copies ran while one was open for 14% of the time, Pallas kernels for 0%

profile of v2, /device:TPU:0, one launch (start us, length us, event | category | flops | bytes accessed | tf_op | source)
XLA Modules:
  0.0 352.6 jit_solution(1765618005103356920)
XLA Ops:
  8.4 1.3 copy.36
  10.1 1.3 fusion.15
  11.6 4.1 %copy.45 = bf16[4096,256]{0,1:T(8,128)(2,1)} copy(bf16[4096,256]{1,0:T(8,128)(2,1)} %param.12) | data formatting | bytes 4194304 | tf_op args[3]
  15.7 4.7 %fusion.16 = (f32[2048,128]{1,0:T(8,128)}, f32[2048,128]{1,0:T(8,128)S(1)}) fusion(f32[128]{0:T(128)S(1)} %fusion.27), kind=kLoop, calls=%fused_computation.24 | loop fusion | flops 262144 | bytes 2097664 | tf_op jit(solution)/shard_map/sin | solution.py:559
  22.6 1.8 tile.8
  24.4 2.4 copy.41
  26.8 2.5 copy.42
  29.3 1.7 tile.20
  31.0 2.4 copy.43
  34.7 1.7 fusion.20.refs_7_
  37.4 4.3 %all-gather.5.cloned.1.call-done = bf16[2,4096,128]{1,0,2:T(2,128)(2,1)} async-done(((bf16[2,4096,32]{1,0,2:T(2,128)(2,1)}), bf16[2,4096,128]{1,0,2:T(2,128)(2,1)}) %all-gather.5.cloned.1.call-update) | async-done | bytes 2097168 | tf_op jit(solution)/shard_map/all_gather | solution.py:575
  41.7 7.4 %fusion.32 = (bf16[1,4096,128]{1,0,2:T(2,128)(2,1)S(1)}, bf16[1,4096,128]{1,0,2:T(2,128)(2,1)}) fusion(bf16[2,4096,128]{1,0,2:T(2,128)(2,1)} %all-gather.5.cloned.1.call-done), kind=kLoop, calls=%fused_computation.49 | loop fusion | bytes 4194304 | tf_op jit(solution)/shard_map/slice | solution.py:578
  49.1 5.0 %copy.51 = bf16[1,4096,128]{2,1,0:T(8,128)(2,1)S(1)} copy(bf16[1,4096,128]{1,0,2:T(2,128)(2,1)} %get-tuple-element.51) | data formatting | bytes 2097152
  54.2 3.6 %copy.50 = bf16[1,4096,128]{2,1,0:T(8,128)(2,1)} copy(bf16[1,4096,128]{1,0,2:T(2,128)(2,1)S(1)} %get-tuple-element.50) | data formatting | bytes 2097152
  57.8 6.0 %pad_maximum_fusion.refs_2_ = bf16[4096,768]{1,0:T(8,128)(2,1)} fusion(bf16[4096,128]{1,0:T(8,128)(2,1)S(1)} %bitcast.27, bf16[4096,128]{1,0:T(8,128)(2,1)} %bitcast.29, bf16[4096,256]{1,0:T(8,128)(2,1)} %collective-permute-done, bf16[4096,256]{1,0:T(8,128)(2,1)} %param.12), kind=kLoop, calls=%fused_computation | loop fusion | flops 25165824 | bytes 12582912 | tf_op jit(solution)/shard_map/concatenate | solution.py:577
  63.8 90.6 %all-gather.3.cloned.1.call-done.refs_5_ = bf16[2048,4096]{1,0:T(8,128)(2,1)} async-done(((bf16[128,4096]{1,0:T(8,128)(2,1)}), bf16[2048,4096]{1,0:T(8,128)(2,1)}) %all-gather.3.cloned.1.call-update) | async-done | bytes 16777232 | tf_op jit(solution)/shard_map/all_gather | solution.py:583
  154.4 12.6 %fusion.6 = f32[2048,512]{1,0:T(8,128)S(1)} fusion(bf16[2048,4096]{1,0:T(8,128)(2,1)} %all-gather.3.cloned.1.call-done.refs_5_, bf16[4096,128]{1,0:T(8,128)(2,1)S(1)} %bitcast.28, bf16[4096,128]{1,0:T(8,128)(2,1)S(1)} %bitcast.30, bf16[4096,256]{1,0:T(8,128)(2,1)} %param.12), kind=kOutput, calls=%fused_computation.7 | convolution fusion | flops 8603566080 | bytes 25165824 | tf_op jit(solution)/shard_map/dot_general | solution.py:587
  170.2 1.9 fusion.10
  174.8 31.0 %attention.1 = (bf16[2048,256]{1,0:T(8,128)(2,1)}, bf16[2048,256]{1,0:T(8,128)(2,1)}, bf16[2048,256]{1,0:T(8,128)(2,1)}) custom-call(bf16[2048,256]{1,0:T(8,128)(2,1)} %slice.58.q_ref, bf16[2048,128]{1,0:T(8,128)(2,1)} %slice.59.k_ref, bf16[2048,128]{1,0:T(8,128)(2,1)} %slice.67.v_ref, bf16[2048,256]{1,0:T(8,128)(2,1)} %bitcast.32, f32[2048,128]{1,0:T(8,128)} %copy-done.3, ...), custom_call_target="tpu_custom_call" | custom-call | tf_op jit(solution)/shard_map/attention/pallas_call | solution.py:132
  205.8 121.3 %back.1 = (bf16[128,4096]{1,0:T(8,128)(2,1)}, bf16[4,2,320,512]{3,2,1,0:T(8,128)(2,1)}, f32[320,512]{1,0:T(8,128)}) custom-call(bf16[8,2,128,256]{3,2,1,0:T(8,128)(2,1)} %bitcast.33, bf16[8,2,128,256]{3,2,1,0:T(8,128)(2,1)} %bitcast.34, bf16[4096,768]{1,0:T(8,128)(2,1)} %pad_maximum_fusion.refs_2_, bf16[128,4096]{1,0:T(8,128)(2,1)} %bitcast.26, ...), custom_call_target="tpu_custom_call" | custom-call | tf_op jit(solution)/shard_map/back/pallas_call | solution.py:538
  327.2 5.3 %copy.46 = bf16[2,4,512,320]{2,1,0,3:T(4,128)(2,1)} copy(bf16[2,4,512,320]{2,3,0,1:T(8,128)(2,1)} %bitcast.31) | data formatting | bytes 5242880 | tf_op jit(solution)/shard_map/transpose | solution.py:610
  332.4 4.3 %reshape.108 = bf16[4096,320]{0,1:T(8,128)(2,1)S(1)} reshape(bf16[2,4,512,320]{2,1,0,3:T(4,128)(2,1)} %copy.46) | data formatting | bytes 5242880 | tf_op jit(solution)/shard_map/reshape | solution.py:610
  336.7 1.5 split.24
  339.7 4.1 %copy.47 = bf16[4096,256]{1,0:T(8,128)(2,1)} copy(bf16[4096,256]{0,1:T(8,128)(2,1)} %split.24) | data formatting | bytes 4194304
  (46 shorter events, 15.6 us)
Async XLA Ops:
  7.2 2.6 copy-start.2
  7.2 2.9 copy-start.10
  7.2 34.5 %all-gather.5.cloned.1.call-start = ((), (), s32[]{:S(2)}) async-start(), calls=%async_computation.1 | async-start | bytes 2621440 | tf_op jit(solution)/shard_map/all_gather | solution.py:575
  9.8 144.6 %all-gather.3.cloned.1.call-start = ((), (), s32[]{:S(2)}) async-start(), calls=%async_computation | async-start | bytes 17825792 | tf_op jit(solution)/shard_map/all_gather | solution.py:583
  11.5 46.3 %collective-permute-start = (bf16[4096,256]{1,0:T(8,128)(2,1)}, bf16[4096,256]{1,0:T(8,128)(2,1)}, u32[]{:S(2)}, u32[]{:S(2)}) collective-permute-start(bf16[4096,256]{1,0:T(8,128)(2,1)} %param.12), channel_id=1, source_target_pairs={{0,1},{1,0},{2,3},{3,2},{4,5},{5,4},{6,7},{7,6},{8,9},{9,8},{10,11... | collective-permute-start | bytes 6291464 | tf_op jit(solution)/shard_map/ppermute | solution.py:576
  20.3 1.0 copy-start.3
  31.0 3.7 %copy-start.6 = (bf16[4096,32]{0,1:T(8,128)(2,1)S(1)}, bf16[4096,32]{0,1:T(8,128)(2,1)}, u32[]{:S(2)}) copy-start(bf16[4096,32]{0,1:T(8,128)(2,1)} %param.14) | copy-start | bytes 786436
  33.4 3.1 copy-start.8
  33.4 3.1 copy-start.9
  57.8 96.6 %copy-start.4 = (bf16[1,4096,128]{2,1,0:T(8,128)(2,1)S(1)}, bf16[1,4096,128]{2,1,0:T(8,128)(2,1)}, u32[]{:S(2)}) copy-start(bf16[1,4096,128]{2,1,0:T(8,128)(2,1)} %copy.50) | copy-start | bytes 3145732
  167.3 1.9 copy-start
  167.3 2.8 copy-start.1
  336.7 2.3 copy-start.7
  339.0 5.8 %copy-start.5 = (bf16[128,4096]{1,0:T(8,128)(2,1)S(1)}, bf16[128,4096]{1,0:T(8,128)(2,1)}, u32[]{:S(2)}) copy-start(bf16[128,4096]{1,0:T(8,128)(2,1)} %get-tuple-element.17) | copy-start | bytes 3145732
Sparse Core Ops, SparseCore 0:
  10.3 31.3 all-gather.4
  44.2 110.1 all-gather.2

commit v3 on v2

--- a/solution.py
+++ b/solution.py
@@ -2,6 +2,7 @@
 
 import jax
 import jax.numpy as jnp
+import numpy as np
 from jax import lax
 from jax.experimental import pallas as pl
 from jax.experimental.pallas import tpu as pltpu
@@ -291,7 +292,10 @@
 
         def body(c, _):
             at = pl.ds(pl.multiple_of(c * step, step), step)
-            out = dotg(left, r["w3"][at, :], NT) * scale
+            out = dotg(left[:, : 2 * HD], r["w_query"][at, :], NT)
+            out = out + dotg(left[:, 2 * HD : 4 * HD], r["w_other"][at, :], NT)
+            out = out + jnp.dot(left[:, 4 * HD :], r["w_head"][:, at], preferred_element_type=F32)
+            out = out * scale
             r["part"][side, :, :, at] = out.astype(BF).reshape(4, rows // 4, step)
             return 0
 
@@ -458,7 +462,7 @@
     finish(second)
 
 
-ROW_NAMES = ("gq", "gkv", "w3", "tokens", "gain", "rows_hbm", "moment", "own")
+ROW_NAMES = ("gq", "gkv", "w_query", "w_other", "w_head", "tokens", "gain", "rows_hbm", "moment", "own")
 OUT_NAMES = ("grad_tokens", "fresh", "next")
 
 
@@ -498,7 +502,7 @@
 ORDER = "rrrr" + "wrwrwrwrwrw"
 
 
-def back(gq, gkv, w3, tokens, gain, rows, moment, own):
+def back(gq, gkv, w_query, w_other, w_head, tokens, gain, rows, moment, own):
     length, width = rows.shape
     columns, share = own.shape
     block = length // 16
@@ -549,20 +553,176 @@
             collective_id=1, has_side_effects=True, vmem_limit_bytes=62 * 1024 * 1024
         ),
         name="back",
-    )(gq, gkv, w3, tokens, gain, rows, moment, own)
+    )(gq, gkv, w_query, w_other, w_head, tokens, gain, rows, moment, own)
+
+
+def front_kernel(names, *refs):
+    r = dict(zip(names, refs))
+    p = place()
+    link = Link(r["send"], r["recv"])
+    core, y, xh = p["core"], p["y"], p["xh"]
+    sib, across = device(core=1 - core), device(xh=1 - xh)
+    up, down = device(y=lax.rem(y + 1, 4)), device(y=lax.rem(y + 3, 4))
+    odd = lax.rem(y, 2)
+    pair = device(y=y + 1 - 2 * odd)
+    greet([sib, across, up, down])
+    rows, kv = r["rows"], r["kv"]
+    block, width = rows.shape[3], rows.shape[4]
+    thin = HD // INNER
+    mine, other = odd * 2 + core, (1 - odd) * 2 + core
+    kv_slots = [link.slot() for _ in range(4)]
+    kv[mine] = r["kv_own"][...]
+    link.start(kv_slots[0], kv.at[mine], kv.at[mine], pair)
+    inputs = r["tokens"][...].astype(F32)
+    reciprocal = lax.rsqrt(jnp.mean(inputs * inputs, axis=1, keepdims=True) + norm_eps)
+    rows[xh, y, core] = (inputs * reciprocal * r["gain"][...]).astype(BF)
+    top, rest = pl.ds(0, LOW), pl.ds(LOW, block - LOW)
+    cut = lambda n: (lambda ref, i: ref.at[pl.ds(0 if i == 0 else n // 2, n // 2)])
+
+    def cross(slot, q, at):
+        link.start(slot, rows.at[xh, q, core, at], rows.at[xh, q, core, at], across)
+
+    def crossed(slot, q, at):
+        link.wait(slot, rows.at[1 - xh, q, core, at], across)
+
+    def to_sib(slot, side, q):
+        link.start(slot, rows.at[side, q, core], rows.at[side, q, core], sib)
+
+    def spread(side, at, n):
+        return ring_spread(link, y, up, down, lambda q: rows.at[side, q, core, at], cut(n))
+
+    top_slot = link.slot()
+    rest_slots = [link.slot() for _ in range(4)]
+    sib_slots = [[link.slot() for _ in range(4)] for _ in range(2)]
+    q0, q1, q2, q3 = y, lax.rem(y + 1, 4), lax.rem(y + 2, 4), lax.rem(y + 3, 4)
+    cross(top_slot, q0, top)
+    b_own = spread(xh, rest, block - LOW)
+    next(b_own)
+    a_own = spread(xh, top, LOW)
+    next(a_own)
+    cross(rest_slots[0], q0, rest)
+    to_sib(sib_slots[0][0], xh, q0)
+    link.start(kv_slots[1], kv.at[mine], kv.at[mine], sib)
+    link.start(kv_slots[3], r["w_query"], r["w_other"], sib)
+    stored = []
+
+    def project(side, q, k):
+        which = (0, 1, 2, 3)[k % 4]
+        link.wait(sib_slots[k // 4][which], rows.at[side, q, 1 - core], sib)
+        copy = pltpu.make_async_copy(rows.at[side, q], r["rows_out"].at[side, q], r["store"].at[k])
+        copy.start()
+        stored.append(copy)
+        acc = r["acc"]
+        acc[...] = jnp.zeros_like(acc)
+        step = 512
+
+        def body(c, _):
+            at = pl.ds(pl.multiple_of(c * step, step), step)
+            part = rows[side, q, :, :, at].reshape(2 * block, step)
+            acc[:, : 2 * HD] += jnp.dot(part, r["w_query"][at, :], preferred_element_type=F32)
+            acc[:, 2 * HD :] += dotg(part, r["kv_out"][:, at], NT)
+            return 0
+
+        lax.fori_loop(0, width // step, body, 0)
+        scale = width ** (-0.5)
+        here = pl.ds(pl.multiple_of((side * 4 + q) * 2 * block, 2 * block), 2 * block)
+        cos, sin = r["cos"][here, :], r["sin"][here, :]
+        for h in range(2):
+            r["query"][here, h * HD : (h + 1) * HD] = rope(
+                acc[:, h * HD : (h + 1) * HD] * scale, cos, sin, 1.0
+            ).astype(BF)
+        r["key"][here, :] = rope(acc[:, 2 * HD : 3 * HD] * scale, cos, sin, 1.0).astype(BF)
+        r["value"][here, :] = (acc[:, 3 * HD :] * scale).astype(BF)
+
+    crossed(top_slot, q0, top)
+    a_far = spread(1 - xh, top, LOW)
+    next(a_far)
+    next(b_own)
+    cross(rest_slots[1], q1, rest)
+    cross(rest_slots[3], q3, rest)
+    next(a_own)
+    to_sib(sib_slots[0][1], xh, q1)
+    to_sib(sib_slots[0][3], xh, q3)
+    link.wait(kv_slots[0], kv.at[other], pair)
+    link.start(kv_slots[2], kv.at[other], kv.at[other], sib)
+    crossed(rest_slots[0], q0, rest)
+    to_sib(sib_slots[1][0], 1 - xh, q0)
+    finish(b_own)
+    cross(rest_slots[2], q2, rest)
+    finish(a_own)
+    to_sib(sib_slots[0][2], xh, q2)
+    next(a_far)
+    link.wait(kv_slots[1], kv.at[odd * 2 + 1 - core], sib)
+    link.wait(kv_slots[2], kv.at[(1 - odd) * 2 + 1 - core], sib)
+    for j in range(INNER):
+        r["kv_out"][j * thin : (j + 1) * thin, :] = kv[j, :thin, :]
+        r["kv_out"][HD + j * thin : HD + (j + 1) * thin, :] = kv[j, thin:, :]
+    project(xh, q0, 0)
+    project(xh, q1, 1)
+    project(xh, q3, 3)
+    project(1 - xh, q0, 4)
+    project(xh, q2, 2)
+    finish(a_far)
+    crossed(rest_slots[1], q1, rest)
+    to_sib(sib_slots[1][1], 1 - xh, q1)
+    crossed(rest_slots[3], q3, rest)
+    to_sib(sib_slots[1][3], 1 - xh, q3)
+    crossed(rest_slots[2], q2, rest)
+    to_sib(sib_slots[1][2], 1 - xh, q2)
+    project(1 - xh, q1, 5)
+    project(1 - xh, q3, 7)
+    project(1 - xh, q2, 6)
+    link.wait(kv_slots[3], r["w_other"], sib)
+    for copy in stored:
+        copy.wait()
+    link.drain()
+
+
+FRONT_IN = ("tokens", "gain", "w_query", "kv_own", "cos", "sin")
+FRONT_OUT = ("query", "key", "value", "rows_out", "w_other", "kv_out")
+
+
+def front(tokens, gain, w_query, kv_own, cos, sin):
+    block, width = tokens.shape
+    length = cos.shape[0]
+    v = pltpu.VMEM
+    shape = jax.ShapeDtypeStruct
+    scratch = dict(
+        rows=v((2, 4, 2, block, width), BF),
+        kv=v((INNER, 2 * HD // INNER, width), BF),
+        acc=v((2 * block, 4 * HD), F32),
+        store=pltpu.SemaphoreType.DMA((8,)),
+        send=pltpu.SemaphoreType.DMA((32,)),
+        recv=pltpu.SemaphoreType.DMA((32,)),
+    )
+    whole = pl.BlockSpec(memory_space=pltpu.VMEM)
+    far = pl.BlockSpec(memory_space=pl.ANY)
+    return pl.pallas_call(
+        functools.partial(front_kernel, FRONT_IN + FRONT_OUT + tuple(scratch)),
+        in_specs=[whole] * len(FRONT_IN),
+        out_specs=[whole, whole, whole, far, far, whole],
+        out_shape=[
+            shape((length, 2 * HD), BF),
+            shape((length, HD), BF),
+            shape((length, HD), BF),
+            shape((2, 4, 2, block, width), BF),
+            shape(w_query.shape, BF),
+            shape((2 * HD, width), BF),
+        ],
+        scratch_shapes=list(scratch.values()),
+        compiler_params=pltpu.CompilerParams(
+            collective_id=2, has_side_effects=True, vmem_limit_bytes=60 * 1024 * 1024
+        ),
+        name="front",
+    )(tokens, gain, w_query, kv_own, cos, sin)
 
 
 def tables(length):
-    within = jnp.arange(HD, dtype=jnp.int32) // 2
-    rates = jnp.power(jnp.float32(rope_base), within.astype(F32) * (-2.0 / HD))
-    angle = jnp.arange(length, dtype=F32)[:, None] * rates[None, :]
-    return jnp.cos(angle), jnp.sin(angle)
-
-
-def rotate(matrix, cos, sin):
-    even = jnp.arange(matrix.shape[1]) % 2 == 0
-    partner = jnp.where(even[None, :], -jnp.roll(matrix, -1, axis=1), jnp.roll(matrix, 1, axis=1))
-    return matrix * cos + partner * sin
+    within = np.arange(HD) // 2
+    rates = np.power(np.float32(rope_base), within.astype(np.float32) * np.float32(-2.0 / HD))
+    angle = np.arange(length, dtype=np.float32)[:, None] * rates.astype(np.float32)[None, :]
+    angle = angle.astype(np.float64)
+    return np.cos(angle).astype(np.float32), np.sin(angle).astype(np.float32)
 
 
 def per_device(
@@ -571,25 +731,14 @@
     query_width = w_query.shape[1]
     key_width = w_key.shape[1]
     width = tokens.shape[2]
-    in_scale = width ** (-0.5)
-    w_head = lax.all_gather(jnp.stack([w_key, w_value]), SHARE, axis=2, tiled=True)
-    w_other = lax.ppermute(w_query, "core", [(0, 1), (1, 0)])
-    w3 = jnp.concatenate([w_query, w_other, w_head[0], w_head[1]], axis=1)
-    w_all = jnp.concatenate([w_query, w_head[0], w_head[1]], axis=1)
-    inputs = tokens[0].astype(F32)
-    reciprocal = lax.rsqrt(jnp.mean(inputs * inputs, axis=1, keepdims=True) + norm_eps)
-    unit_rows = inputs * reciprocal
-    normed = (unit_rows * gain).astype(BF)
-    normed_all = lax.all_gather(normed, TENSOR, axis=0, tiled=True)
-    length = normed_all.shape[0]
-    cos, sin = tables(length)
-    cos3, sin3 = jnp.tile(cos, (1, 3)), jnp.tile(sin, (1, 3))
-    projected = jnp.dot(normed_all, w_all, preferred_element_type=F32) * in_scale
-    turned = rotate(projected[:, : 3 * HD], cos3, sin3).astype(BF)
-    values = projected[:, 3 * HD :].astype(BF)
-    attended, grad_query, grad_kv = attention(
-        turned[:, : 2 * HD], turned[:, 2 * HD :], values, cotangent[0], cos, sin
-    )
+    cos, sin = tables(cotangent.shape[1])
+    kv_own = jnp.concatenate([w_key, w_value], axis=1).T
+    query, key, value, rows, w_other, w_head = front(
+        tokens[0], gain[None], w_query, kv_own, cos, sin
+    )
+    length = query.shape[0]
+    rows = rows.reshape(length, width)
+    attended, grad_query, grad_kv = attention(query, key, value, cotangent[0], cos, sin)
     dp_rank = lax.axis_index(DP)
     share = moment_query.shape[0]
     w_mine = jnp.concatenate([w_query, w_key, w_value], axis=1)
@@ -599,10 +748,12 @@
     grad_tokens, fresh, moved = back(
         grad_query.reshape(by_block),
         grad_kv.reshape(by_block),
-        w3,
+        w_query,
+        w_other,
+        w_head,
         tokens[0],
         gain[None],
-        normed_all,
+        rows,
         moment,
         own,
     )

time: 353 us -> 275 us (0.78)
  waiting for transfers between devices: 94.9 us -> 0 us
  Pallas kernels: 152 us -> 243 us
  local copies, waits for them, and re-layouts: 60.4 us -> 24.8 us
  between operations: 14.2 us -> 0.7 us
  matrix products: 12.6 us -> 0 us
  other arithmetic: 17.9 us -> 5.46 us
    all_gather x2 -> x0, waiting for transfers between devices: 94.9 us -> none  [the longest x1 90.6 us: per_device(): normed_all = lax.all_gather(normed, TENSOR, axis=0, tiled=True)]
    pallas_call x0 -> x1, Pallas kernels: none -> 90.5 us  [front(): pl.pallas_call(functools.partial(front_kernel, FRONT_IN + FRONT_OUT + tup...]
    dot_general x1 -> x0, matrix products: 12.6 us -> none  [per_device(): jnp.dot(normed_all, w_all, preferred_element_type=F32) * in_scale]
    unnamed x29 -> x13, local copies, waits for them, and re-layouts: 22.8 us -> 10.4 us
    slice x6 -> x0, local copies, waits for them, and re-layouts: 11.7 us -> none  [the longest x1 7.44 us: per_device(): w_all = jnp.concatenate([w_query, w_head[0], w_head[1]], axis=1)]
    another operation x5 -> x0, local copies, waits for them, and re-layouts: 9.56 us -> none  [the longest x4 8.23 us: per_device(): cos3, sin3 = (jnp.tile(cos, (1, 3)), jnp.tile(sin, (1, 3)))]
    concatenate x1 -> x0, other arithmetic: 6.01 us -> none  [per_device(): w3 = jnp.concatenate([w_query, w_other, w_head[0], w_head[1]], axis=1)]
    sin x1 -> x0, other arithmetic: 4.65 us -> none  [tables(): return (jnp.cos(angle), jnp.sin(angle))]
  transfers between devices with their start and end apart: 3 -> 0, of which waited for: 2 -> 0; matrix products, arithmetic and copies ran while one was open for 14% -> 0% of each run, Pallas kernels for 0% -> 0%
where the time goes in v3:
time: 275 us; the launch traced here: 274 us
  Pallas kernels  243 us (88%)
  local copies, waits for them, and re-layouts  24.8 us (9%)
  other arithmetic  5.46 us (2%)
    pallas_call x1, Pallas kernels, back(): pl.pallas_call(functools.partial(back_kernel, names), in_specs=[pl.BlockS...  122 us
    pallas_call x1, Pallas kernels, front(): pl.pallas_call(functools.partial(front_kernel, FRONT_IN + FRONT_OUT + tup...  90.5 us
    pallas_call x1, Pallas kernels, attention(): pl.pallas_call(functools.partial(attn_kernel, BQ, TC, HD ** (-0.5)), grid...  31 us
    unnamed x13, local copies, waits for them, and re-layouts  10.4 us

profile of v3, /device:TPU:0, one launch (start us, length us, event | category | flops | bytes accessed | tf_op | source)
XLA Modules:
  0.0 274.0 jit_solution(2666467570584771575)
XLA Ops:
  0.6 0.0 copy-start
  0.7 1.4 copy.23
  2.0 1.8 maximum_bitcast_fusion.refs_8_
  3.9 0.0 copy-start.2
  3.9 0.0 copy-start.3
  3.9 1.9 maximum_bitcast_fusion.1.refs_3_
  5.8 0.0 copy-done
  5.8 2.8 %copy.24 = bf16[4096,256]{0,1:T(8,128)(2,1)} copy(bf16[4096,256]{1,0:T(8,128)(2,1)S(1)} %copy-done) | data formatting | bytes 4194304 | tf_op args[3]
  8.6 0.0 copy-done.2
  8.6 0.0 copy-done.3
  8.6 1.7 fusion.2.refs_9_
  10.4 90.5 %front.1 = (bf16[2048,256]{1,0:T(8,128)(2,1)}, bf16[2048,128]{1,0:T(8,128)(2,1)}, bf16[2048,128]{1,0:T(8,128)(2,1)}, bf16[2,4,2,128,4096]{4,3,2,1,0:T(8,128)(2,1...) custom-call(bf16[128,4096]{1,0:T(8,128)(2,1)} %bitcast.19, f32[1,4096]{1,0:T(1,128)} %bitcast.28, ...), custom_call_target="tpu_custom_call" | custom-call | tf_op jit(solution)/shard_map/front/pallas_call | solution.py:700
  100.9 31.0 %attention.1 = (bf16[2048,256]{1,0:T(8,128)(2,1)}, bf16[2048,256]{1,0:T(8,128)(2,1)}, bf16[2048,256]{1,0:T(8,128)(2,1)}) custom-call(bf16[2048,256]{1,0:T(8,128)(2,1)} %get-tuple-element.20.q_ref, bf16[2048,128]{1,0:T(8,128)(2,1)} %get-tuple-element.21.k_ref, bf16[2048,128]{1,0:T(8,128)(2,1)} %get-tuple-element.22.v_ref, bf16[2048,256]{1,0:T(8,128)(2,1)} %bitcast.22, ...), custom_call_target="tpu_custom_call" | custom-call | tf_op jit(solution)/shard_map/attention/pallas_call | solution.py:133
  131.9 121.5 %back.1 = (bf16[128,4096]{1,0:T(8,128)(2,1)}, bf16[4,2,320,512]{3,2,1,0:T(8,128)(2,1)}, f32[320,512]{1,0:T(8,128)}) custom-call(bf16[8,2,128,256]{3,2,1,0:T(8,128)(2,1)} %bitcast.23, bf16[8,2,128,256]{3,2,1,0:T(8,128)(2,1)} %bitcast.24, bf16[4096,256]{1,0:T(8,128)(2,1)} %refs_2_.3, bf16[4096,256]{1,0:T(8,128)(2,1)} %get-tuple-element.26.refs_3_, ...), custom_call_target="tpu_custom_call" | custom-call | tf_op jit(solution)/shard_map/back/pallas_call | solution.py:542
  253.4 5.3 %copy.25 = bf16[2,4,512,320]{2,1,0,3:T(4,128)(2,1)} copy(bf16[2,4,512,320]{2,3,0,1:T(8,128)(2,1)} %bitcast.21) | data formatting | bytes 5242880 | tf_op jit(solution)/shard_map/transpose | solution.py:761
  258.7 4.3 %reshape.31 = bf16[4096,320]{0,1:T(8,128)(2,1)S(1)} reshape(bf16[2,4,512,320]{2,1,0,3:T(4,128)(2,1)} %copy.25) | data formatting | bytes 5242880 | tf_op jit(solution)/shard_map/reshape | solution.py:761
  263.0 1.5 fusion.4
  264.5 1.1 split.27
  265.6 1.0 copy.27
  266.6 0.8 fusion.3
  267.4 1.5 split.24
  268.9 4.2 %copy.26 = bf16[4096,256]{1,0:T(8,128)(2,1)} copy(bf16[4096,256]{0,1:T(8,128)(2,1)} %split.24) | data formatting | bytes 4194304
  273.0 0.0 copy-done.1
  273.1 1.0 copy.29
  (1 shorter events, 0.0 us)
Async XLA Ops:
  0.6 5.2 %copy-start = (bf16[4096,256]{1,0:T(8,128)(2,1)S(1)}, bf16[4096,256]{1,0:T(8,128)(2,1)}, u32[]{:S(2)}) copy-start(bf16[4096,256]{1,0:T(8,128)(2,1)} %refs_2_.3) | copy-start | bytes 6291460
  3.9 4.8 %copy-start.2 = (bf16[4096,32]{0,1:T(8,128)(2,1)S(1)}, bf16[4096,32]{0,1:T(8,128)(2,1)}, u32[]{:S(2)}) copy-start(bf16[4096,32]{0,1:T(8,128)(2,1)} %param.16) | copy-start | bytes 786436
  3.9 4.8 %copy-start.3 = (bf16[4096,32]{0,1:T(8,128)(2,1)S(1)}, bf16[4096,32]{0,1:T(8,128)(2,1)}, u32[]{:S(2)}) copy-start(bf16[4096,32]{0,1:T(8,128)(2,1)} %param.15) | copy-start | bytes 786436
  268.9 4.2 %copy-start.1 = (bf16[128,4096]{1,0:T(8,128)(2,1)S(1)}, bf16[128,4096]{1,0:T(8,128)(2,1)}, u32[]{:S(2)}) copy-start(bf16[128,4096]{1,0:T(8,128)(2,1)} %get-tuple-element.29) | copy-start | bytes 3145732

commit v4 on v3

v4 whole, which is shorter than its diff:
```python
import functools
from types import SimpleNamespace

import jax
import jax.numpy as jnp
import numpy as np
from jax import lax
from jax.experimental import pallas as pl
from jax.experimental.pallas import tpu as pltpu
from jax.sharding import Mesh
from jax.sharding import PartitionSpec as P

D = 4096
HEADS = 32
KVH = 4
HD = 128
F32 = jnp.float32
BF = jnp.bfloat16
CHIPS = ("x", "yh", "yl")
TENSOR = ("x", "yh", "yl", "core")
SHARE = ("yl", "core")
DP = ("dp_0", "dp_1")
ALL = ("dp_0", "dp_1", "x", "yh", "yl", "core")

rope_base = 1000000.0
norm_eps = 1e-06
stat_eps = 1e-06
learn_rate = 0.05
keep_rate = 0.9


def rope(x, cos, sin, sign):
    lane = lax.broadcasted_iota(jnp.int32, x.shape, 1)
    nxt = pltpu.roll(x, x.shape[1]-1, 1)
    prv = pltpu.roll(x, 1, 1)
    partner = jnp.where(lane % 2 == 0, -nxt, prv)
    return x*cos + partner*(sin*sign)

NT=(((1,),(1,)),((),()))
TN=(((0,),(0,)),((),()))
def dotg(a,b,dims):
    return lax.dot_general(a,b,dims,preferred_element_type=F32)

def attn_kernel(BQ, TC, hs, q_ref, k_ref, v_ref, do_ref, cos_ref, sin_ref,
                out_ref, gq_ref, gkv_ref, va, s_scr, r_scr, p_scr, dk, dv, m_scr, o_scr, g_scr):
    i = pl.program_id(0)
    n = pl.num_programs(0)
    T = k_ref.shape[0]
    R = 2*BQ
    @pl.when(i == 0)
    def _():
        va[:, :HD] = v_ref[...]
        va[:, HD:] = jnp.ones((T, HD), BF)
        dk[...] = jnp.zeros_like(dk)
        dv[...] = jnp.zeros_like(dv)
    q = jnp.concatenate([q_ref[:, :HD], q_ref[:, HD:]], axis=0)
    do = jnp.concatenate([do_ref[:, :HD], do_ref[:, HD:]], axis=0)
    first = i*BQ
    full = first // TC
    used = (first + BQ + TC - 1)//TC
    m_scr[...] = jnp.full((R, HD), -3e38, F32)
    def lane_max(s):
        m = m_scr[...]
        for j in range(TC//HD):
            m = jnp.maximum(m, s[:, j*HD:(j+1)*HD])
        m_scr[...] = m
    def scores(c):
        ks = k_ref[pl.ds(pl.multiple_of(c*TC, TC), TC), :]
        vs = v_ref[pl.ds(pl.multiple_of(c*TC, TC), TC), :]
        r_scr[c] = dotg(do, vs, NT)
        return dotg(q, ks, NT)
    def body1(c, _):
        s = scores(c)
        s_scr[c] = s
        lane_max(s)
        return 0
    lax.fori_loop(0, full, body1, 0)
    def body1d(c, _):
        s = scores(c)
        row = first + lax.broadcasted_iota(jnp.int32, (R, TC), 0) % BQ
        col = c*TC + lax.broadcasted_iota(jnp.int32, (R, TC), 1)
        s = jnp.where(row >= col, s, -1e30)
        s_scr[c] = s
        lane_max(s)
        return 0
    lax.fori_loop(full, used, body1d, 0)
    c2 = hs * 1.4426950408889634
    m = jnp.max(m_scr[...], axis=1, keepdims=True)
    mb = jnp.broadcast_to(m * c2, (R, HD))
    o_scr[...] = jnp.zeros_like(o_scr)
    def body2(c, _):
        s = s_scr[c]
        p = jnp.concatenate([jnp.exp2(s[:, j*HD:(j+1)*HD]*c2 - mb) for j in range(TC//HD)], axis=1).astype(BF)
        p_scr[c] = p
        o_scr[...] += jnp.dot(p, va[pl.ds(pl.multiple_of(c*TC, TC), TC), :], preferred_element_type=F32)
        return 0
    lax.fori_loop(0, used, body2, 0)
    inv = 1.0 / o_scr[:, HD:]
    o = o_scr[:, :HD] * inv
    out_ref[:, :HD] = o[:BQ].astype(BF)
    out_ref[:, HD:] = o[BQ:].astype(BF)
    dof = do.astype(F32)
    delta = jnp.broadcast_to(jnp.sum(dof*o, axis=1, keepdims=True), (R, HD))
    qn = (q.astype(F32) * (inv*hs)).astype(BF)
    don = (dof*inv).astype(BF)
    g_scr[...] = jnp.zeros_like(g_scr)
    def body3(c, _):
        at = pl.ds(pl.multiple_of(c*TC, TC), TC)
        p = p_scr[c]
        r = r_scr[c]
        pf = p.astype(F32)
        g = jnp.concatenate([pf[:, j*HD:(j+1)*HD]*(r[:, j*HD:(j+1)*HD] - delta) for j in range(TC//HD)], axis=1).astype(BF)
        g_scr[...] += jnp.dot(g, k_ref[at, :], preferred_element_type=F32)
        dk[at, :] += dotg(g, qn, TN)
        dv[at, :] += dotg(p, don, TN)
        return 0
    lax.fori_loop(0, used, body3, 0)
    gq = g_scr[...] * (inv*hs)
    here = pl.ds(pl.multiple_of(first, BQ), BQ)
    cos = cos_ref[here, :]
    sin = sin_ref[here, :]
    gq_ref[:, :HD] = rope(gq[:BQ], cos, sin, -1.0).astype(BF)
    gq_ref[:, HD:] = rope(gq[BQ:], cos, sin, -1.0).astype(BF)
    @pl.when(i == n-1)
    def _():
        gkv_ref[:, :HD] = rope(dk[...], cos_ref[...], sin_ref[...], -1.0).astype(BF)
        gkv_ref[:, HD:] = dv[...].astype(BF)

def attention(q, k, v, do, cos, sin, BQ=512, TC=512):
    T = q.shape[0]
    R = 2*BQ
    whole = pl.BlockSpec((T, HD), lambda i: (0, 0))
    rows = pl.BlockSpec((BQ, 2*HD), lambda i: (i, 0))
    return pl.pallas_call(
        functools.partial(attn_kernel, BQ, TC, HD**-0.5),
        grid=(T//BQ,),
        in_specs=[rows, whole, whole, rows, whole, whole],
        out_specs=[rows, rows, pl.BlockSpec((T, 2*HD), lambda i: (0, 0))],
        out_shape=[jax.ShapeDtypeStruct((T, 2*HD), BF)]*3,
        scratch_shapes=[pltpu.VMEM((T, 2*HD), BF), pltpu.VMEM((T//TC, R, TC), F32), pltpu.VMEM((T//TC, R, TC), F32),
            pltpu.VMEM((T//TC, R, TC), BF), pltpu.VMEM((T, HD), F32), pltpu.VMEM((T, HD), F32),
            pltpu.VMEM((R, HD), F32), pltpu.VMEM((R, 2*HD), F32), pltpu.VMEM((R, HD), F32)],
        compiler_params=pltpu.CompilerParams(vmem_limit_bytes=56*1024*1024),
        name="attention",
    )(q, k, v, do, cos, sin)


MESH_ID = pl.DeviceIdType.MESH
INNER = 4


def place():
    at = lax.axis_index
    return SimpleNamespace(
        xl=at("dp_0"), z=at("dp_1"), xh=at("x"), y=at("yh") * 2 + at("yl"), core=at("core")
    )


def device(**moved):
    names = {}
    for key, value in moved.items():
        if key == "y":
            names["yh"] = value // 2
            names["yl"] = value % 2
        elif key == "x":
            names["x"] = value // 2
            names["dp_0"] = value % 2
        else:
            names[{"xl": "dp_0", "z": "dp_1", "xh": "x", "core": "core"}[key]] = value
    return names


class Link:
    def __init__(self, send, recv):
        self.send, self.recv, self.used, self.sent = send, recv, 0, []

    def slot(self):
        self.used += 1
        return self.used - 1

    def start(self, slot, src, dst, to):
        copy = pltpu.make_async_remote_copy(
            src_ref=src,
            dst_ref=dst,
            send_sem=self.send.at[slot],
            recv_sem=self.recv.at[slot],
            device_id=to,
            device_id_type=MESH_ID,
        )
        copy.start()
        self.sent.append(copy)

    def wait(self, slot, landed, to):
        pltpu.make_async_remote_copy(
            src_ref=landed,
            dst_ref=landed,
            send_sem=self.send.at[slot],
            recv_sem=self.recv.at[slot],
            device_id=to,
            device_id_type=MESH_ID,
        ).wait_recv()

    def drain(self):
        for copy in self.sent:
            copy.wait_send()


def added(ref, other):
    ref[...] = (ref[...].astype(F32) + other[...].astype(F32)).astype(BF)


def ring_reduce(link, me, up, down, piece, half, part_low, part_high, full_low, full_high):
    s = [link.slot() for _ in range(4)]
    far = piece(lax.rem(me + 2, 4))
    link.start(s[0], half(far, 0), part_low, up)
    link.start(s[1], half(far, 1), part_high, down)
    yield
    above = piece(lax.rem(me + 1, 4))
    link.wait(s[0], part_low, down)
    added(half(above, 0), part_low)
    link.start(s[2], above, full_low, up)
    below = piece(lax.rem(me + 3, 4))
    link.wait(s[1], part_high, up)
    added(half(below, 1), part_high)
    link.start(s[3], below, full_high, down)
    yield
    link.wait(s[2], full_low, down)
    link.wait(s[3], full_high, up)


def ring_spread(link, me, up, down, piece, half):
    s = [link.slot() for _ in range(4)]
    mine = piece(me)
    link.start(s[0], mine, mine, up)
    link.start(s[1], mine, mine, down)
    yield
    low, high = piece(lax.rem(me + 3, 4)), piece(lax.rem(me + 1, 4))
    link.wait(s[0], low, down)
    link.start(s[2], half(low, 0), half(low, 0), up)
    link.wait(s[1], high, up)
    link.start(s[3], half(high, 1), half(high, 1), down)
    yield
    far = piece(lax.rem(me + 2, 4))
    link.wait(s[2], half(far, 0), down)
    link.wait(s[3], half(far, 1), up)


def finish(steps):
    for _ in steps:
        pass


def greet(others):
    barrier = pltpu.get_barrier_semaphore()
    for other in others:
        pl.semaphore_signal(barrier, inc=1, device_id=other, device_id_type=MESH_ID)
    pl.semaphore_wait(barrier, len(others))


def cut_at(n, lower):
    return n // 32 * 16 if lower else n - n // 32 * 16


def cut(n, lower):
    at = cut_at(n, lower)
    return lambda ref, i: ref.at[pl.ds(0, at) if i == 0 else pl.ds(at, n - at)]


LOW_FRONT = 64
LOW_BACK = 80


def rows_chain(r, link, p):
    core, y, xh = p.core, p.y, p.xh
    sib, across = device(core=1 - core), device(xh=1 - xh)
    up, down = device(y=lax.rem(y + 1, 4)), device(y=lax.rem(y + 3, 4))
    near = y + 1 - 2 * lax.rem(y, 2)
    pair = device(y=near)
    gq, gkv, sib_q, sib_kv, cat = r.gq, r.gkv, r.sib_q, r.sib_kv, r.cat
    one, two = link.slot(), link.slot()
    link.start(one, gkv.at[:, 1 - core], sib_kv, sib)
    link.start(two, gq.at[:, 1 - core], sib_q, sib)
    yield
    link.wait(one, sib_kv, sib)
    added(sib_kv, gkv.at[:, core])
    three = link.slot()
    odd = lax.rem(y, 2)
    half = HD // 2

    def columns(first):
        picks = [sib_kv[:, :, at + first : at + first + half] for at in (0, HD)]
        return jnp.concatenate(picks, axis=2)

    low, high_half = columns(0), columns(half)
    r.kv_out[...] = jnp.where(odd == 1, low, high_half)
    r.kv_keep[...] = jnp.where(odd == 1, high_half, low)
    link.start(three, r.kv_out, r.pair_kv, pair)
    link.wait(two, sib_q, sib)
    cat[:, :, : 2 * HD] = gq[:, core]
    cat[:, :, 2 * HD : 4 * HD] = sib_q[...]
    cat[:, :, 4 * HD :] = sib_kv[...]
    rows = 4 * cat.shape[1]
    width = r.part.shape[3]
    step = 512
    scale = width ** (-0.5)

    def products(side):
        left = cat[pl.ds(side * 4, 4)].reshape(rows, 6 * HD)

        def body(c, _):
            at = pl.ds(pl.multiple_of(c * step, step), step)
            out = dotg(left[:, : 2 * HD], r.w_query[at, :], NT)
            out = out + dotg(left[:, 2 * HD : 4 * HD], r.w_other[at, :], NT)
            out = out + jnp.dot(left[:, 4 * HD :], r.w_head[:, at], preferred_element_type=F32)
            out = out * scale
            r.part[side, :, :, at] = out.astype(BF).reshape(4, rows // 4, step)
            return 0

        lax.fori_loop(0, width // step, body, 0)

    part = r.part
    high = part.shape[2] - LOW_BACK
    top, rest = pl.ds(0, LOW_BACK), pl.ds(LOW_BACK, high)

    def ring(side, rows_at, n, bufs):
        return ring_reduce(
            link, y, up, down, lambda q: part.at[side, q, rows_at], cut(n, rows_at is rest), *bufs
        )

    def bufs(k):
        n = (LOW_BACK, LOW_BACK, high)[k]
        first = cut_at(n, k == 2)
        sizes = (first, n - first, n, n)
        refs = (r.part_low, r.part_high, r.full_low, r.full_high)
        return tuple(ref.at[k, pl.ds(0, size)] for ref, size in zip(refs, sizes))

    products(1 - xh)
    across_slots = [link.slot() for _ in range(4)]
    order = [lax.rem(y + i, 4) for i in (2, 1, 3, 0)]
    for i, q in enumerate(order):
        link.start(across_slots[i], part.at[1 - xh, q, rest], r.cross.at[q], across)
    far_ring = ring(1 - xh, top, LOW_BACK, bufs(0))
    next(far_ring)
    products(xh)
    near_ring = ring(xh, top, LOW_BACK, bufs(1))
    next(near_ring)
    yield
    link.wait(three, r.pair_kv, pair)
    total = (r.kv_keep[...].astype(F32) + r.pair_kv[...].astype(F32)).astype(BF)
    r.kv_all[:, core] = total
    four = link.slot()
    link.start(four, r.kv_all.at[:, core], r.kv_all.at[:, core], sib)
    next(far_ring)
    link.wait(four, r.kv_all.at[:, 1 - core], sib)
    yield
    next(near_ring)
    yield
    finish(far_ring)
    k = 0
    done = part.at[1 - xh, y, top]
    done[...] = (
        done[...].astype(F32)
        + r.full_low[k, :LOW_BACK].astype(F32)
        + r.full_high[k, :LOW_BACK].astype(F32)
    ).astype(BF)
    last = link.slot()
    link.start(last, done, r.cross_top, across)
    yield
    def crossed(i):
        link.wait(across_slots[i], r.cross.at[order[i]], across)
        added(part.at[xh, order[i], rest], r.cross.at[order[i]])

    crossed(0)
    rest_ring = ring(xh, rest, high, bufs(2))
    next(rest_ring)
    yield
    crossed(1)
    crossed(2)
    finish(near_ring)
    next(rest_ring)
    yield
    crossed(3)
    finish(rest_ring)
    link.wait(last, r.cross_top, across)
    own = part.at[xh, y]
    top_rows = (
        own[top].astype(F32)
        + r.full_low[1, :LOW_BACK].astype(F32)
        + r.full_high[1, :LOW_BACK].astype(F32)
        + r.cross_top[...].astype(F32)
    )
    rest_rows = (
        own[rest].astype(F32)
        + r.full_low[2, :high].astype(F32)
        + r.full_high[2, :high].astype(F32)
    )
    for first, grad_normed in ((0, top_rows), (LOW_BACK, rest_rows)):
        at = pl.ds(first, grad_normed.shape[0])
        inputs = r.tokens[at, :].astype(F32)
        reciprocal = lax.rsqrt(jnp.mean(inputs * inputs, axis=1, keepdims=True) + norm_eps)
        unit = inputs * reciprocal
        grad_unit = grad_normed * r.gain[...]
        inner = jnp.mean(grad_unit * unit, axis=1, keepdims=True)
        r.grad_tokens[at, :] = (reciprocal * (grad_unit - unit * inner)).astype(BF)


def weight_chain(r, link, p):
    core, y, xh, xl, z = p.core, p.y, p.xh, p.xl, p.z
    up, down = device(z=lax.rem(z + 1, 4)), device(z=lax.rem(z + 3, 4))
    beside = device(xl=1 - xl)
    wide = 2 * HD
    thin = HD // INNER
    length = r.turned.shape[1]
    share = r.rows.shape[2]
    width = 8 * share
    scale = width ** (-0.5)
    index = lambda ref, i: ref.at[i]
    chains = ("q", "kv")

    def ring(n):
        grad = getattr(r, n + "_grad")
        bufs = [getattr(r, n + end) for end in ("_low", "_high", "_full_low", "_full_high")]
        return ring_reduce(link, z, up, down, lambda q: grad.at[q], index, *bufs)

    r.turned[...] = r.gq[...].reshape(length, wide).T

    def query_part(c, _):
        r.arrive(c)
        out = jnp.dot(r.turned[...], r.rows[c], preferred_element_type=F32) * scale
        r.q_grad[lax.rem(c, 4), c // 4] = out.T.astype(BF)
        return 0

    lax.fori_loop(0, 8, query_part, 0)
    rings = {"q": ring("q")}
    next(rings["q"])
    yield
    which = pl.multiple_of(core * thin, thin)
    r.turned[:HD, :] = r.kv_all[...].reshape(length, HD).T
    r.kv_turned[:thin, :] = r.turned[pl.ds(which, thin), :]
    r.kv_turned[thin:, :] = r.turned[pl.ds(which + HD // 2, thin), :]

    def kv_part(c, _):
        out = jnp.dot(r.kv_turned[...], r.rows[c], preferred_element_type=F32) * scale
        r.kv_grad[lax.rem(c, 4), c // 4] = out.astype(BF)
        return 0

    lax.fori_loop(0, 8, kv_part, 0)
    rings["kv"] = ring("kv")
    next(rings["kv"])
    yield
    next(rings["q"])
    yield
    next(rings["kv"])
    yield
    slots = {}
    for n in chains:
        finish(rings[n])
        mine = getattr(r, n + "_grad").at[z]
        for i in range(2):
            mine[i] = (
                mine[i].astype(F32)
                + getattr(r, n + "_full_low")[i].astype(F32)
                + getattr(r, n + "_full_high")[i].astype(F32)
            ).astype(BF)
        slots[n] = link.slot()
        link.start(slots[n], mine.at[1 - xl], getattr(r, n + "_beside"), beside)
    yield
    square = jnp.zeros((1, 1), F32)
    for n in chains:
        link.wait(slots[n], getattr(r, n + "_beside"), beside)
        summed = getattr(r, n + "_grad")[z, xl].astype(F32) + getattr(r, n + "_beside")[...].astype(F32)
        getattr(r, n + "_summed")[...] = summed
        part = jnp.sum(summed * summed, axis=0, keepdims=True)
        square = square + jnp.sum(part, axis=1, keepdims=True)
    x = xh * 2 + xl
    stages = (
        [device(core=1 - core)],
        [device(x=lax.rem(x + i, 4)) for i in (1, 2, 3)],
        [device(y=lax.rem(y + i, 4)) for i in (1, 2, 3)],
        [device(z=lax.rem(z + i, 4)) for i in (1, 2, 3)],
    )
    total = jnp.broadcast_to(square, (8, HD))
    for k, others in enumerate(stages):
        r.square[k] = total
        slot = [link.slot() for _ in others]
        for i, other in enumerate(others):
            link.start(slot[i], r.square.at[k], r.squares.at[k, i], other)
        yield
        for i, other in enumerate(others):
            link.wait(slot[i], r.squares.at[k, i], other)
            total = total + r.squares[k, i]
    count_all = 1.0 * D * HD * (HEADS + 2 * KVH)
    factor = lax.rsqrt(total[:1, :1] / count_all + stat_eps)

    def place_of(q, side):
        return pl.ds(pl.multiple_of((side * 4 + q) * share, share), share)

    here = place_of(z, xl)
    moved = keep_rate * r.moment_q[...] + r.q_summed[...] * factor
    r.next_q[...] = moved
    r.fresh_q[here, :] = (r.w_query[here, :].astype(F32) - learn_rate * moved).astype(BF)
    views = {"q": lambda q, side: r.fresh_q.at[place_of(q, side)]}
    cuts = {"q": lambda ref, i: ref.at[pl.ds(i * share // 2, share // 2)]}
    moved = keep_rate * r.moment_kv[...] + r.kv_summed[...] * factor
    r.next_kv[...] = moved
    r.fresh_kv[:, here] = (r.kv_own[:, here].astype(F32) - learn_rate * moved).astype(BF)
    views["kv"] = lambda q, side: r.fresh_kv.at[:, place_of(q, side)]
    cuts["kv"] = lambda ref, i: ref.at[pl.ds(i * thin, thin)]

    def spread(n, side):
        return ring_spread(link, z, up, down, lambda q: views[n](q, side), cuts[n])

    first, second = [], []
    for n in chains:
        slots[n] = link.slot()
        link.start(slots[n], views[n](z, xl), views[n](z, xl), beside)
        first.append(spread(n, xl))
        next(first[-1])
    yield
    for n in chains:
        link.wait(slots[n], views[n](z, 1 - xl), beside)
        second.append(spread(n, 1 - xl))
        next(second[-1])
    yield
    for s in first:
        next(s)
    yield
    for s in second:
        next(s)
    yield
    for s in first + second:
        finish(s)


def back_kernel(names, *refs):
    r = SimpleNamespace(**dict(zip(names, refs)))
    p = place()
    link = Link(r.send, r.recv)
    step = r.rows.shape[2]
    for c in range(8):
        pltpu.make_async_copy(
            r.rows_hbm.at[:, pl.ds(c * step, step)], r.rows.at[c], r.load.at[c]
        ).start()

    def arrive(c):
        pltpu.make_async_copy(
            r.rows_hbm.at[:, pl.ds(pl.multiple_of(c * step, step), step)], r.rows.at[c], r.load.at[c]
        ).wait()

    r.arrive = arrive
    x = p.xh * 2 + p.xl
    others = [device(core=1 - p.core)]
    for i in (1, 2, 3):
        others.append(device(x=lax.rem(x + i, 4)))
        others.append(device(y=lax.rem(p.y + i, 4)))
        others.append(device(z=lax.rem(p.z + i, 4)))
    greet(others)
    rows, weights = rows_chain(r, link, p), weight_chain(r, link, p)
    for which in ORDER:
        next(rows if which == "r" else weights, None)
    finish(rows)
    finish(weights)
    link.drain()


ORDER = "rwrrwwwrwrwwrwwrwwrww"


def back(gq, gkv, w_query, w_other, w_head, kv_own, tokens, gain, rows, moment_q, moment_kv):
    length, width = rows.shape
    share, wide = moment_q.shape
    few = moment_kv.shape[0]
    block = length // 16
    most = max(LOW_BACK, block - LOW_BACK)
    v = pltpu.VMEM
    shape = jax.ShapeDtypeStruct
    ins = dict(
        gq=gq,
        gkv=gkv,
        w_query=w_query,
        w_other=w_other,
        w_head=w_head,
        kv_own=kv_own,
        tokens=tokens,
        gain=gain,
        rows_hbm=rows,
        moment_q=moment_q,
        moment_kv=moment_kv,
    )
    outs = dict(
        grad_tokens=shape((block, width), BF),
        fresh_q=shape(w_query.shape, BF),
        fresh_kv=shape((few, width), BF),
        next_q=shape(moment_q.shape, F32),
        next_kv=shape(moment_kv.shape, F32),
    )
    scratch = dict(
        sib_q=v((8, block, wide), BF),
        sib_kv=v((8, block, wide), BF),
        pair_kv=v((8, block, HD), BF),
        kv_out=v((8, block, HD), BF),
        kv_keep=v((8, block, HD), BF),
        kv_all=v((8, 2, block, HD), BF),
        cat=v((8, block, 3 * wide), BF),
        part=v((2, 4, block, width), BF),
        part_low=v((3, most // 32 * 16 + 16, width), BF),
        part_high=v((3, most // 32 * 16 + 16, width), BF),
        full_low=v((3, most, width), BF),
        full_high=v((3, most, width), BF),
        cross=v((4, block - LOW_BACK, width), BF),
        cross_top=v((LOW_BACK, width), BF),
        rows=v((8, length, share), BF),
        load=pltpu.SemaphoreType.DMA((8,)),
        turned=v((wide, length), BF),
        kv_turned=v((few, length), BF),
        square=v((4, 8, HD), F32),
        squares=v((4, 3, 8, HD), F32),
        send=pltpu.SemaphoreType.DMA((64,)),
        recv=pltpu.SemaphoreType.DMA((64,)),
    )
    for n, dims in (("q", (share, wide)), ("kv", (few, share))):
        scratch[n + "_grad"] = v((4, 2, *dims), BF)
        scratch[n + "_low"] = v(dims, BF)
        scratch[n + "_high"] = v(dims, BF)
        scratch[n + "_full_low"] = v((2, *dims), BF)
        scratch[n + "_full_high"] = v((2, *dims), BF)
        scratch[n + "_beside"] = v(dims, BF)
        scratch[n + "_summed"] = v(dims, F32)
    whole = pl.BlockSpec(memory_space=pltpu.VMEM)
    far = pl.BlockSpec(memory_space=pl.ANY)
    return pl.pallas_call(
        functools.partial(back_kernel, tuple(ins) + tuple(outs) + tuple(scratch)),
        in_specs=[far if n == "rows_hbm" else whole for n in ins],
        out_specs=[whole] * len(outs),
        out_shape=list(outs.values()),
        scratch_shapes=list(scratch.values()),
        compiler_params=pltpu.CompilerParams(
            collective_id=1, has_side_effects=True, vmem_limit_bytes=62 * 1024 * 1024
        ),
        name="back",
    )(*ins.values())

def front_kernel(names, *refs):
    r = SimpleNamespace(**dict(zip(names, refs)))
    p = place()
    link = Link(r.send, r.recv)
    core, y, xh = p.core, p.y, p.xh
    sib, across = device(core=1 - core), device(xh=1 - xh)
    up, down = device(y=lax.rem(y + 1, 4)), device(y=lax.rem(y + 3, 4))
    odd = lax.rem(y, 2)
    pair = device(y=y + 1 - 2 * odd)
    z = p.z
    z_up, z_down = device(z=lax.rem(z + 1, 4)), device(z=lax.rem(z + 3, 4))
    greet([sib, across, up, down, z_up, z_down])
    rows, kv = r.rows, r.kv
    block, width = rows.shape[3], rows.shape[4]
    thin = HD // INNER
    mine, other = odd * 2 + core, (1 - odd) * 2 + core
    kv_slots = [link.slot() for _ in range(4)]
    quarter = kv.shape[1] // 4

    def kv_piece(which):
        return lambda q: kv.at[which, pl.ds(pl.multiple_of(q * quarter, quarter), quarter)]

    kv[mine] = r.kv_own[...]
    link.start(kv_slots[0], kv_piece(mine)(z), kv_piece(mine)(z), pair)
    inputs = r.tokens[...].astype(F32)
    reciprocal = lax.rsqrt(jnp.mean(inputs * inputs, axis=1, keepdims=True) + norm_eps)
    rows[xh, y, core] = (inputs * reciprocal * r.gain[...]).astype(BF)
    top, rest = pl.ds(0, LOW_FRONT), pl.ds(LOW_FRONT, block - LOW_FRONT)

    def cross(slot, q, at):
        link.start(slot, rows.at[xh, q, core, at], rows.at[xh, q, core, at], across)

    def crossed(slot, q, at):
        link.wait(slot, rows.at[1 - xh, q, core, at], across)

    def to_sib(slot, side, q):
        link.start(slot, rows.at[side, q, core], rows.at[side, q, core], sib)

    def spread(side, at, n):
        return ring_spread(link, y, up, down, lambda q: rows.at[side, q, core, at], cut(n, at is rest))

    top_slot = link.slot()
    rest_slots = [link.slot() for _ in range(4)]
    sib_slots = [[link.slot() for _ in range(4)] for _ in range(2)]
    q0, q1, q2, q3 = y, lax.rem(y + 1, 4), lax.rem(y + 2, 4), lax.rem(y + 3, 4)
    cross(top_slot, q0, top)
    b_own = spread(xh, rest, block - LOW_FRONT)
    next(b_own)
    a_own = spread(xh, top, LOW_FRONT)
    next(a_own)
    cross(rest_slots[0], q0, rest)
    to_sib(sib_slots[0][0], xh, q0)
    link.start(kv_slots[1], kv.at[mine], kv.at[mine], sib)
    link.start(kv_slots[3], r.w_query, r.w_other, sib)
    stored = []

    def project(side, q, k):
        which = (0, 1, 2, 3)[k % 4]
        link.wait(sib_slots[k // 4][which], rows.at[side, q, 1 - core], sib)
        copy = pltpu.make_async_copy(rows.at[side, q], r.rows_out.at[side, q], r.store.at[k])
        copy.start()
        stored.append(copy)
        acc = r.acc
        acc[...] = jnp.zeros_like(acc)
        step = 512

        def body(c, _):
            at = pl.ds(pl.multiple_of(c * step, step), step)
            part = rows[side, q, :, :, at].reshape(2 * block, step)
            acc[:, : 2 * HD] += jnp.dot(part, r.w_query[at, :], preferred_element_type=F32)
            acc[:, 2 * HD :] += dotg(part, r.kv_out[:, at], NT)
            return 0

        lax.fori_loop(0, width // step, body, 0)
        scale = width ** (-0.5)
        here = pl.ds(pl.multiple_of((side * 4 + q) * 2 * block, 2 * block), 2 * block)
        cos, sin = r.cos[here, :], r.sin[here, :]
        for h in range(2):
            r.query[here, h * HD : (h + 1) * HD] = rope(
                acc[:, h * HD : (h + 1) * HD] * scale, cos, sin, 1.0
            ).astype(BF)
        r.key[here, :] = rope(acc[:, 2 * HD : 3 * HD] * scale, cos, sin, 1.0).astype(BF)
        r.value[here, :] = (acc[:, 3 * HD :] * scale).astype(BF)

    link.wait(kv_slots[0], kv_piece(other)(z), pair)
    sides = lambda ref, i: ref.at[:, pl.ds(i * (width // 2), width // 2)]
    kv_ring = ring_spread(link, z, z_up, z_down, kv_piece(other), sides)
    next(kv_ring)
    next(kv_ring)
    finish(kv_ring)
    link.start(kv_slots[2], kv.at[other], kv.at[other], sib)
    crossed(top_slot, q0, top)
    a_far = spread(1 - xh, top, LOW_FRONT)
    next(a_far)
    next(b_own)
    cross(rest_slots[1], q1, rest)
    cross(rest_slots[3], q3, rest)
    next(a_own)
    to_sib(sib_slots[0][1], xh, q1)
    to_sib(sib_slots[0][3], xh, q3)
    crossed(rest_slots[0], q0, rest)
    to_sib(sib_slots[1][0], 1 - xh, q0)
    finish(b_own)
    cross(rest_slots[2], q2, rest)
    finish(a_own)
    to_sib(sib_slots[0][2], xh, q2)
    next(a_far)
    link.wait(kv_slots[1], kv.at[odd * 2 + 1 - core], sib)
    link.wait(kv_slots[2], kv.at[(1 - odd) * 2 + 1 - core], sib)
    for j in range(INNER):
        r.kv_out[j * thin : (j + 1) * thin, :] = kv[j, :thin, :]
        r.kv_out[HD + j * thin : HD + (j + 1) * thin, :] = kv[j, thin:, :]
    project(xh, q0, 0)
    project(xh, q1, 1)
    project(xh, q3, 3)
    project(1 - xh, q0, 4)
    project(xh, q2, 2)
    finish(a_far)
    crossed(rest_slots[1], q1, rest)
    to_sib(sib_slots[1][1], 1 - xh, q1)
    crossed(rest_slots[3], q3, rest)
    to_sib(sib_slots[1][3], 1 - xh, q3)
    crossed(rest_slots[2], q2, rest)
    to_sib(sib_slots[1][2], 1 - xh, q2)
    project(1 - xh, q1, 5)
    project(1 - xh, q3, 7)
    project(1 - xh, q2, 6)
    link.wait(kv_slots[3], r.w_other, sib)
    for copy in stored:
        copy.wait()
    link.drain()


def front(tokens, gain, w_query, kv_own, cos, sin):
    block, width = tokens.shape
    length = cos.shape[0]
    v = pltpu.VMEM
    shape = jax.ShapeDtypeStruct
    ins = dict(tokens=tokens, gain=gain, w_query=w_query, kv_own=kv_own, cos=cos, sin=sin)
    outs = dict(
        query=shape((length, 2 * HD), BF),
        key=shape((length, HD), BF),
        value=shape((length, HD), BF),
        rows_out=shape((2, 4, 2, block, width), BF),
        w_other=shape(w_query.shape, BF),
        kv_out=shape((2 * HD, width), BF),
    )
    scratch = dict(
        rows=v((2, 4, 2, block, width), BF),
        kv=v((INNER, 2 * HD // INNER, width), BF),
        acc=v((2 * block, 4 * HD), F32),
        store=pltpu.SemaphoreType.DMA((8,)),
        send=pltpu.SemaphoreType.DMA((40,)),
        recv=pltpu.SemaphoreType.DMA((40,)),
    )
    whole = pl.BlockSpec(memory_space=pltpu.VMEM)
    far = pl.BlockSpec(memory_space=pl.ANY)
    return pl.pallas_call(
        functools.partial(front_kernel, tuple(ins) + tuple(outs) + tuple(scratch)),
        in_specs=[whole] * len(ins),
        out_specs=[whole, whole, whole, far, far, whole],
        out_shape=list(outs.values()),
        scratch_shapes=list(scratch.values()),
        compiler_params=pltpu.CompilerParams(
            collective_id=2, has_side_effects=True, vmem_limit_bytes=60 * 1024 * 1024
        ),
        name="front",
    )(*ins.values())


def tables(length):
    within = np.arange(HD) // 2
    rates = np.power(np.float32(rope_base), within.astype(np.float32) * np.float32(-2.0 / HD))
    angle = np.arange(length, dtype=np.float32)[:, None] * rates.astype(np.float32)[None, :]
    angle = angle.astype(np.float64)
    return np.cos(angle).astype(np.float32), np.sin(angle).astype(np.float32)


def per_device(
    tokens, cotangent, gain, w_query, w_key, w_value, moment_query, moment_key, moment_value
):
    key_width = w_key.shape[1]
    width = tokens.shape[2]
    cos, sin = tables(cotangent.shape[1])
    kv_own = jnp.concatenate([w_key, w_value], axis=1).T
    query, key, value, rows, w_other, w_head = front(
        tokens[0], gain[None], w_query, kv_own, cos, sin
    )
    length = query.shape[0]
    rows = rows.reshape(length, width)
    attended, grad_query, grad_kv = attention(query, key, value, cotangent[0], cos, sin)
    by_block = (8, 2, length // 16, 2 * HD)
    grad_tokens, fresh_query, fresh_kv, next_query, next_kv = back(
        grad_query.reshape(by_block),
        grad_kv.reshape(by_block),
        w_query,
        w_other,
        w_head,
        kv_own,
        tokens[0],
        gain[None],
        rows,
        moment_query,
        jnp.concatenate([moment_key, moment_value], axis=1).T,
    )
    fresh_key, fresh_value = fresh_kv[:key_width].T, fresh_kv[key_width:].T
    next_key, next_value = next_kv[:key_width].T, next_kv[key_width:].T
    return (
        attended[None],
        grad_tokens[None],
        fresh_query,
        fresh_key,
        fresh_value,
        next_query,
        next_key,
        next_value,
    )


def solution(mesh):
    torus = Mesh(mesh.devices.reshape(2, 4, 2, 2, 2, 2), ALL)
    placed = (
        P(DP, TENSOR, None),
        P(DP, None, TENSOR),
        P(),
        P(None, TENSOR),
        P(None, TENSOR),
        P(None, TENSOR),
        P(DP, TENSOR),
        P(DP, TENSOR),
        P(DP, TENSOR),
    )
    return jax.shard_map(
        per_device,
        mesh=torus,
        in_specs=placed,
        out_specs=(
            P(DP, None, TENSOR),
            P(DP, TENSOR, None),
            P(None, TENSOR),
            P(None, TENSOR),
            P(None, TENSOR),
            P(DP, TENSOR),
            P(DP, TENSOR),
            P(DP, TENSOR),
        ),
        check_vma=False,
    )
```

time: 275 us -> 237 us (0.86)
  Pallas kernels: 243 us -> 224 us
  local copies, waits for them, and re-layouts: 24.8 us -> 8.01 us
    pallas_call x2, Pallas kernels: 212 us -> 193 us  [the longest x1 110 us: back(): pl.pallas_call(functools.partial(back_kernel, tuple(ins) + tuple(outs) +...]
    unnamed x13 -> x7, local copies, waits for them, and re-layouts: 10.4 us -> 4.48 us
    split x4 -> x0, local copies, waits for them, and re-layouts: 4.91 us -> none  [the longest x2 2.6 us: per_device(): next_query, next_key, next_value = jnp.split(moved, ends, axis=1)]
    reshape x1 -> x0, local copies, waits for them, and re-layouts: 4.26 us -> none  [per_device(): fresh = fresh.transpose(1, 0, 3, 2).reshape(width, -1)]
where the time goes in v4:
time: 237 us; the launch traced here: 236 us
  Pallas kernels  224 us (95%)
  local copies, waits for them, and re-layouts  8.01 us (3%)
  other arithmetic  3.39 us (1%)
    pallas_call x1, Pallas kernels, back(): pl.pallas_call(functools.partial(back_kernel, tuple(ins) + tuple(outs) +...  110 us
    pallas_call x1, Pallas kernels, front(): pl.pallas_call(functools.partial(front_kernel, tuple(ins) + tuple(outs) +...  83.2 us
    pallas_call x1, Pallas kernels, attention(): pl.pallas_call(functools.partial(attn_kernel, BQ, TC, HD ** (-0.5)), grid...  31 us

profile of v4, /device:TPU:0, one launch (start us, length us, event | category | flops | bytes accessed | tf_op | source)
XLA Modules:
  0.0 236.3 jit_solution(9163646356739001551)
XLA Ops:
  0.6 1.5 maximum_bitcast_fusion.1.refs_10_
  2.2 1.9 maximum_bitcast_fusion.refs_3_.refs_5_
  4.0 83.2 %front.1 = (bf16[2048,256]{1,0:T(8,128)(2,1)}, bf16[2048,128]{1,0:T(8,128)(2,1)}, bf16[2048,128]{1,0:T(8,128)(2,1)}, bf16[2,4,2,128,4096]{4,3,2,1,0:T(8,128)(2,1...) custom-call(bf16[128,4096]{1,0:T(8,128)(2,1)} %bitcast.21, f32[1,4096]{1,0:T(1,128)} %bitcast.27, ...), custom_call_target="tpu_custom_call" | custom-call | tf_op jit(solution)/shard_map/front/pallas_call | solution.py:800
  87.2 31.0 %attention.1 = (bf16[2048,256]{1,0:T(8,128)(2,1)}, bf16[2048,256]{1,0:T(8,128)(2,1)}, bf16[2048,256]{1,0:T(8,128)(2,1)}) custom-call(bf16[2048,256]{1,0:T(8,128)(2,1)} %get-tuple-element.22.q_ref, bf16[2048,128]{1,0:T(8,128)(2,1)} %get-tuple-element.23.k_ref, bf16[2048,128]{1,0:T(8,128)(2,1)} %get-tuple-element.24.v_ref, bf16[2048,256]{1,0:T(8,128)(2,1)} %bitcast.23, ...), custom_call_target="tpu_custom_call" | custom-call | tf_op jit(solution)/shard_map/attention/pallas_call | solution.py:134
  118.3 110.0 %back.1 = (bf16[128,4096]{1,0:T(8,128)(2,1)}, bf16[4096,256]{1,0:T(8,128)(2,1)}, bf16[64,4096]{1,0:T(8,128)(2,1)}, f32[512,256]{1,0:T(8,128)}, f32[64,512]{1,0:T(8,128)}) custom-call(bf16[8,2,128,256]{3,2,1,0:T(8,128)(2,1)} %bitcast.24, bf16[8,2,128,256]{3,2,1,0:T(8,128)(2,1)} %bitcast.25, bf16[4096,256]{1,0:T(8,128)(2,1)} %refs_2_.3, ...), custom_call_target="tpu_custom_call" | custom-call | tf_op jit(solution)/shard_map/back/pallas_call | solution.py:631
  228.3 0.0 copy-start
  228.3 1.7 slice_bitcast_fusion.2
  230.0 1.9 slice_bitcast_fusion
  231.9 2.3 copy.22
  234.1 0.0 copy-done
  234.1 0.0 copy-start.1
  234.1 1.3 copy.23
  235.5 0.1 copy-done.1
  235.5 0.8 copy.24
Async XLA Ops:
  228.3 5.8 %copy-start = (bf16[4096,256]{1,0:T(8,128)(2,1)S(1)}, bf16[4096,256]{1,0:T(8,128)(2,1)}, u32[]{:S(2)}) copy-start(bf16[4096,256]{1,0:T(8,128)(2,1)} %get-tuple-element.50) | copy-start | bytes 6291460
  234.1 1.4 copy-start.1

commit v5 on v4

--- a/solution.py
+++ b/solution.py
@@ -276,7 +276,8 @@
     up, down = device(y=lax.rem(y + 1, 4)), device(y=lax.rem(y + 3, 4))
     near = y + 1 - 2 * lax.rem(y, 2)
     pair = device(y=near)
-    gq, gkv, sib_q, sib_kv, cat = r.gq, r.gkv, r.sib_q, r.sib_kv, r.cat
+    gq, gkv, sib_kv, cat = r.gq, r.gkv, r.sib_kv, r.cat
+    sib_q = cat.at[:, :, pl.ds(2 * HD, 2 * HD)]
     one, two = link.slot(), link.slot()
     link.start(one, gkv.at[:, 1 - core], sib_kv, sib)
     link.start(two, gq.at[:, 1 - core], sib_q, sib)
@@ -297,7 +298,6 @@
     link.start(three, r.kv_out, r.pair_kv, pair)
     link.wait(two, sib_q, sib)
     cat[:, :, : 2 * HD] = gq[:, core]
-    cat[:, :, 2 * HD : 4 * HD] = sib_q[...]
     cat[:, :, 4 * HD :] = sib_kv[...]
     rows = 4 * cat.shape[1]
     width = r.part.shape[3]
@@ -327,12 +327,10 @@
             link, y, up, down, lambda q: part.at[side, q, rows_at], cut(n, rows_at is rest), *bufs
         )
 
+    names = ("part_low", "part_high", "full_low", "full_high")
+
     def bufs(k):
-        n = (LOW_BACK, LOW_BACK, high)[k]
-        first = cut_at(n, k == 2)
-        sizes = (first, n - first, n, n)
-        refs = (r.part_low, r.part_high, r.full_low, r.full_high)
-        return tuple(ref.at[k, pl.ds(0, size)] for ref, size in zip(refs, sizes))
+        return [getattr(r, name + str(k)) for name in names]
 
     products(1 - xh)
     across_slots = [link.slot() for _ in range(4)]
@@ -356,12 +354,11 @@
     next(near_ring)
     yield
     finish(far_ring)
-    k = 0
     done = part.at[1 - xh, y, top]
     done[...] = (
         done[...].astype(F32)
-        + r.full_low[k, :LOW_BACK].astype(F32)
-        + r.full_high[k, :LOW_BACK].astype(F32)
+        + r.full_low0[...].astype(F32)
+        + r.full_high0[...].astype(F32)
     ).astype(BF)
     last = link.slot()
     link.start(last, done, r.cross_top, across)
@@ -385,14 +382,14 @@
     own = part.at[xh, y]
     top_rows = (
         own[top].astype(F32)
-        + r.full_low[1, :LOW_BACK].astype(F32)
-        + r.full_high[1, :LOW_BACK].astype(F32)
+        + r.full_low1[...].astype(F32)
+        + r.full_high1[...].astype(F32)
         + r.cross_top[...].astype(F32)
     )
     rest_rows = (
         own[rest].astype(F32)
-        + r.full_low[2, :high].astype(F32)
-        + r.full_high[2, :high].astype(F32)
+        + r.full_low2[...].astype(F32)
+        + r.full_high2[...].astype(F32)
     )
     for first, grad_normed in ((0, top_rows), (LOW_BACK, rest_rows)):
         at = pl.ds(first, grad_normed.shape[0])
@@ -434,6 +431,8 @@
     rings = {"q": ring("q")}
     next(rings["q"])
     yield
+    next(rings["q"])
+    yield
     which = pl.multiple_of(core * thin, thin)
     r.turned[:HD, :] = r.kv_all[...].reshape(length, HD).T
     r.kv_turned[:thin, :] = r.turned[pl.ds(which, thin), :]
@@ -448,12 +447,11 @@
     rings["kv"] = ring("kv")
     next(rings["kv"])
     yield
-    next(rings["q"])
-    yield
-    next(rings["kv"])
-    yield
     slots = {}
     for n in chains:
+        if n == "kv":
+            next(rings[n])
+            yield
         finish(rings[n])
         mine = getattr(r, n + "_grad").at[z]
         for i in range(2):
@@ -464,7 +462,7 @@
             ).astype(BF)
         slots[n] = link.slot()
         link.start(slots[n], mine.at[1 - xl], getattr(r, n + "_beside"), beside)
-    yield
+        yield
     square = jnp.zeros((1, 1), F32)
     for n in chains:
         link.wait(slots[n], getattr(r, n + "_beside"), beside)
@@ -479,57 +477,84 @@
         [device(y=lax.rem(y + i, 4)) for i in (1, 2, 3)],
         [device(z=lax.rem(z + i, 4)) for i in (1, 2, 3)],
     )
+    def place_of(q, side):
+        return pl.ds(pl.multiple_of((side * 4 + q) * share, share), share)
+
+    here = place_of(z, xl)
+    r.fresh_q[here, :] = r.q_summed[...].astype(BF)
+    r.fresh_kv[:, here] = r.kv_summed[...].astype(BF)
+    views = dict(
+        q=lambda q, side: r.fresh_q.at[place_of(q, side)],
+        kv=lambda q, side: r.fresh_kv.at[:, place_of(q, side)],
+    )
+    cuts = dict(
+        q=lambda ref, i: ref.at[pl.ds(i * share // 2, share // 2)],
+        kv=lambda ref, i: ref.at[pl.ds(i * thin, thin)],
+    )
+
+    def spread(side):
+        return [
+            ring_spread(sums, z, up, down, functools.partial(views[n], side=side), cuts[n])
+            for n in chains
+        ]
+
     total = jnp.broadcast_to(square, (8, HD))
+    sums = Link(r.send_sum, r.recv_sum)
+    first, second = spread(xl), spread(1 - xl)
     for k, others in enumerate(stages):
         r.square[k] = total
         slot = [link.slot() for _ in others]
         for i, other in enumerate(others):
             link.start(slot[i], r.square.at[k], r.squares.at[k, i], other)
+        if k == 0:
+            for n in chains:
+                slots[n] = sums.slot()
+                sums.start(slots[n], views[n](z, xl), views[n](z, xl), beside)
+            for ring_steps in first:
+                next(ring_steps)
+        if k == 2:
+            for n in chains:
+                sums.wait(slots[n], views[n](z, 1 - xl), beside)
+            for ring_steps in second:
+                next(ring_steps)
+        if k == 3:
+            for ring_steps in first:
+                next(ring_steps)
         yield
         for i, other in enumerate(others):
-            link.wait(slot[i], r.squares.at[k, i], other)
+            back = others[len(others) - 1 - i]
+            link.wait(slot[i], r.squares.at[k, i], back)
             total = total + r.squares[k, i]
+    for ring_steps in second:
+        next(ring_steps)
     count_all = 1.0 * D * HD * (HEADS + 2 * KVH)
     factor = lax.rsqrt(total[:1, :1] / count_all + stat_eps)
-
-    def place_of(q, side):
-        return pl.ds(pl.multiple_of((side * 4 + q) * share, share), share)
-
-    here = place_of(z, xl)
-    moved = keep_rate * r.moment_q[...] + r.q_summed[...] * factor
-    r.next_q[...] = moved
-    r.fresh_q[here, :] = (r.w_query[here, :].astype(F32) - learn_rate * moved).astype(BF)
-    views = {"q": lambda q, side: r.fresh_q.at[place_of(q, side)]}
-    cuts = {"q": lambda ref, i: ref.at[pl.ds(i * share // 2, share // 2)]}
-    moved = keep_rate * r.moment_kv[...] + r.kv_summed[...] * factor
-    r.next_kv[...] = moved
-    r.fresh_kv[:, here] = (r.kv_own[:, here].astype(F32) - learn_rate * moved).astype(BF)
-    views["kv"] = lambda q, side: r.fresh_kv.at[:, place_of(q, side)]
-    cuts["kv"] = lambda ref, i: ref.at[pl.ds(i * thin, thin)]
-
-    def spread(n, side):
-        return ring_spread(link, z, up, down, lambda q: views[n](q, side), cuts[n])
-
-    first, second = [], []
-    for n in chains:
-        slots[n] = link.slot()
-        link.start(slots[n], views[n](z, xl), views[n](z, xl), beside)
-        first.append(spread(n, xl))
-        next(first[-1])
-    yield
-    for n in chains:
-        link.wait(slots[n], views[n](z, 1 - xl), beside)
-        second.append(spread(n, 1 - xl))
-        next(second[-1])
-    yield
-    for s in first:
-        next(s)
-    yield
-    for s in second:
-        next(s)
-    yield
-    for s in first + second:
-        finish(s)
+    r.next_q[...] = keep_rate * r.moment_q[...] + r.q_summed[...] * factor
+    r.next_kv[...] = keep_rate * r.moment_kv[...] + r.kv_summed[...] * factor
+    few = r.fresh_kv.shape[0]
+
+    def update(side):
+        def body(q, _):
+            at = place_of(q, side)
+            moment = r.moment_all[side * 4 + q].astype(F32)
+            moved = keep_rate * moment[:share] + r.fresh_q[at, :].astype(F32) * factor
+            r.fresh_q[at, :] = (r.w_query[at, :].astype(F32) - learn_rate * moved).astype(BF)
+            moment = jnp.concatenate([moment[share : share + few], moment[share + few :]], axis=1)
+            moved = keep_rate * moment + r.fresh_kv[:, at].astype(F32) * factor
+            r.fresh_kv[:, at] = (r.kv_own[:, at].astype(F32) - learn_rate * moved).astype(BF)
+            return 0
+
+        lax.fori_loop(0, 4, body, 0)
+
+    yield
+    for ring_steps in first:
+        finish(ring_steps)
+    yield
+    for ring_steps in second:
+        finish(ring_steps)
+    sums.drain()
+    update(xl)
+    update(1 - xl)
 
 
 def back_kernel(names, *refs):
@@ -563,15 +588,16 @@
     link.drain()
 
 
-ORDER = "rwrrwwwrwrwwrwwrwwrww"
-
-
-def back(gq, gkv, w_query, w_other, w_head, kv_own, tokens, gain, rows, moment_q, moment_kv):
+ORDER = "rwrwrwrwwwwwwwrrwwrw"
+
+
+def back(
+    gq, gkv, w_query, w_other, w_head, kv_own, tokens, gain, rows, moment_q, moment_kv, moment_all
+):
     length, width = rows.shape
     share, wide = moment_q.shape
     few = moment_kv.shape[0]
     block = length // 16
-    most = max(LOW_BACK, block - LOW_BACK)
     v = pltpu.VMEM
     shape = jax.ShapeDtypeStruct
     ins = dict(
@@ -586,6 +612,7 @@
         rows_hbm=rows,
         moment_q=moment_q,
         moment_kv=moment_kv,
+        moment_all=moment_all,
     )
     outs = dict(
         grad_tokens=shape((block, width), BF),
@@ -595,7 +622,6 @@
         next_kv=shape(moment_kv.shape, F32),
     )
     scratch = dict(
-        sib_q=v((8, block, wide), BF),
         sib_kv=v((8, block, wide), BF),
         pair_kv=v((8, block, HD), BF),
         kv_out=v((8, block, HD), BF),
@@ -603,21 +629,25 @@
         kv_all=v((8, 2, block, HD), BF),
         cat=v((8, block, 3 * wide), BF),
         part=v((2, 4, block, width), BF),
-        part_low=v((3, most // 32 * 16 + 16, width), BF),
-        part_high=v((3, most // 32 * 16 + 16, width), BF),
-        full_low=v((3, most, width), BF),
-        full_high=v((3, most, width), BF),
         cross=v((4, block - LOW_BACK, width), BF),
         cross_top=v((LOW_BACK, width), BF),
         rows=v((8, length, share), BF),
         load=pltpu.SemaphoreType.DMA((8,)),
         turned=v((wide, length), BF),
         kv_turned=v((few, length), BF),
+        send_sum=pltpu.SemaphoreType.DMA((20,)),
+        recv_sum=pltpu.SemaphoreType.DMA((20,)),
         square=v((4, 8, HD), F32),
         squares=v((4, 3, 8, HD), F32),
         send=pltpu.SemaphoreType.DMA((64,)),
         recv=pltpu.SemaphoreType.DMA((64,)),
     )
+    for k, n in enumerate((LOW_BACK, LOW_BACK, block - LOW_BACK)):
+        first = cut_at(n, k == 2)
+        scratch["part_low" + str(k)] = v((first, width), BF)
+        scratch["part_high" + str(k)] = v((n - first, width), BF)
+        scratch["full_low" + str(k)] = v((n, width), BF)
+        scratch["full_high" + str(k)] = v((n, width), BF)
     for n, dims in (("q", (share, wide)), ("kv", (few, share))):
         scratch[n + "_grad"] = v((4, 2, *dims), BF)
         scratch[n + "_low"] = v(dims, BF)
@@ -825,6 +855,10 @@
     width = tokens.shape[2]
     cos, sin = tables(cotangent.shape[1])
     kv_own = jnp.concatenate([w_key, w_value], axis=1).T
+    moment_kv = jnp.concatenate([moment_key, moment_value], axis=1).T
+    halves = jnp.split(moment_kv, 2, axis=1)
+    moment_own = jnp.concatenate([moment_query, *halves], axis=0).astype(BF)
+    moment_all = lax.all_gather(moment_own, DP)
     query, key, value, rows, w_other, w_head = front(
         tokens[0], gain[None], w_query, kv_own, cos, sin
     )
@@ -843,7 +877,8 @@
         gain[None],
         rows,
         moment_query,
-        jnp.concatenate([moment_key, moment_value], axis=1).T,
+        moment_kv,
+        moment_all,
     )
     fresh_key, fresh_value = fresh_kv[:key_width].T, fresh_kv[key_width:].T
     next_key, next_value = next_kv[:key_width].T, next_kv[key_width:].T

time: 237 us -> 256 us (1.080)
  between operations: 0.67 us -> 14.1 us
  Pallas kernels: 224 us -> 229 us
    pallas_call x1, Pallas kernels: 83.2 us -> 103 us  [front(): pl.pallas_call(functools.partial(front_kernel, tuple(ins) + tuple(outs) +...]
    pallas_call x1, Pallas kernels: 110 us -> 95.2 us  [back(): pl.pallas_call(functools.partial(back_kernel, tuple(ins) + tuple(outs) +...]
  transfers between devices with their start and end apart: 0 -> 1, of which waited for: 0 -> 0; matrix products, arithmetic and copies ran while one was open for 0% -> 1% of each run, Pallas kernels for 0% -> 52%
where the time goes in v5:
time: 256 us
  Pallas kernels  229 us (89%)
  between operations  14.1 us (6%)
  local copies, waits for them, and re-layouts  8.04 us (3%)
  other arithmetic  4.28 us (2%)
    pallas_call x1, Pallas kernels, front(): pl.pallas_call(functools.partial(front_kernel, tuple(ins) + tuple(outs) +...  103 us
    pallas_call x1, Pallas kernels, back(): pl.pallas_call(functools.partial(back_kernel, tuple(ins) + tuple(outs) +...  95.2 us
    pallas_call x1, Pallas kernels, attention(): pl.pallas_call(functools.partial(attn_kernel, BQ, TC, HD ** (-0.5)), grid...  31.1 us
  transfers between devices with their start and end apart: 1, of which 0 were waited for; matrix products, arithmetic and copies ran while one was open for 1% of the time, Pallas kernels for 52%

profile of v5, /device:TPU:0, one launch (start us, length us, event | category | flops | bytes accessed | tf_op | source)
XLA Modules:
  0.0 255.7 jit_solution(10928075099071591473)
XLA Ops:
  7.2 0.0 copy-start.4
  7.2 0.0 copy-start.5
  7.2 0.0 all-gather.2.cloned.1.call-start
  7.2 0.9 fusion
  8.2 1.1 convert_bitcast_fusion
  9.3 0.8 pad_maximum_fusion
  10.0 0.0 all-gather.2.cloned.1.call-update
  10.1 0.0 copy-done.4
  10.1 0.0 copy-done.5
  10.1 0.8 maximum_bitcast_fusion.refs_3_.refs_5_
  10.9 102.9 %front.1 = (bf16[2048,256]{1,0:T(8,128)(2,1)}, bf16[2048,128]{1,0:T(8,128)(2,1)}, bf16[2048,128]{1,0:T(8,128)(2,1)}, bf16[2,4,2,128,4096]{4,3,2,1,0:T(8,128)(2,1...) custom-call(bf16[128,4096]{1,0:T(8,128)(2,1)} %bitcast.29, f32[1,4096]{1,0:T(1,128)} %bitcast.35, ...), custom_call_target="tpu_custom_call" | custom-call | tf_op jit(solution)/shard_map/front/pallas_call | solution.py:830
  113.8 0.0 copy-start.2
  113.8 0.0 copy-start.3
  113.9 31.1 %attention.1 = (bf16[2048,256]{1,0:T(8,128)(2,1)}, bf16[2048,256]{1,0:T(8,128)(2,1)}, bf16[2048,256]{1,0:T(8,128)(2,1)}) custom-call(bf16[2048,256]{1,0:T(8,128)(2,1)} %get-tuple-element.22.q_ref, bf16[2048,128]{1,0:T(8,128)(2,1)} %get-tuple-element.23.k_ref, bf16[2048,128]{1,0:T(8,128)(2,1)} %get-tuple-element.24.v_ref, bf16[2048,256]{1,0:T(8,128)(2,1)} %bitcast.31, ...), custom_call_target="tpu_custom_call" | custom-call | tf_op jit(solution)/shard_map/attention/pallas_call | solution.py:134
  144.9 0.0 copy-done.2
  144.9 0.7 maximum_bitcast_fusion.1.refs_10_
  145.6 95.2 %back.1 = (bf16[128,4096]{1,0:T(8,128)(2,1)}, bf16[4096,256]{1,0:T(8,128)(2,1)}, bf16[64,4096]{1,0:T(8,128)(2,1)}, f32[512,256]{1,0:T(8,128)}, f32[64,512]{1,0:T(8,128)}) custom-call(bf16[8,2,128,256]{3,2,1,0:T(8,128)(2,1)} %bitcast.32, bf16[8,2,128,256]{3,2,1,0:T(8,128)(2,1)} %bitcast.33, bf16[4096,256]{1,0:T(8,128)(2,1)} %refs_2_.3, ...), custom_call_target="tpu_custom_call" | custom-call | tf_op jit(solution)/shard_map/back/pallas_call | solution.py:661
  240.9 0.0 copy-start
  240.9 1.7 slice_bitcast_fusion.2
  242.5 1.9 slice_bitcast_fusion
  244.4 2.3 copy.22
  246.7 1.3 copy.23
  248.0 0.1 copy-done.1
  248.1 0.8 copy.24
  (5 shorter events, 0.0 us)
Async XLA Ops:
  7.2 2.9 %copy-start.4 = (bf16[4096,32]{0,1:T(8,128)(2,1)S(1)}, bf16[4096,32]{0,1:T(8,128)(2,1)}, u32[]{:S(2)}) copy-start(bf16[4096,32]{0,1:T(8,128)(2,1)} %param.16) | copy-start | bytes 786436
  7.2 2.9 %copy-start.5 = (bf16[4096,32]{0,1:T(8,128)(2,1)S(1)}, bf16[4096,32]{0,1:T(8,128)(2,1)}, u32[]{:S(2)}) copy-start(bf16[4096,32]{0,1:T(8,128)(2,1)} %param.15) | copy-start | bytes 786436
  7.2 138.4 %all-gather.2.cloned.1.call-start = ((), (), s32[]{:S(2)}) async-start(), calls=%async_computation | async-start | bytes 2949120 | tf_op jit(solution)/shard_map/all_gather | solution.py:861
  113.8 31.1 %copy-start.2 = (f32[512,32]{0,1:T(8,128)S(1)}, f32[512,32]{0,1:T(8,128)}, u32[]{:S(2)}) copy-start(f32[512,32]{0,1:T(8,128)} %param.19) | copy-start | bytes 196612
  113.8 31.1 %copy-start.3 = (f32[512,32]{0,1:T(8,128)S(1)}, f32[512,32]{0,1:T(8,128)}, u32[]{:S(2)}) copy-start(f32[512,32]{0,1:T(8,128)} %param.18) | copy-start | bytes 196612
  240.9 5.8 %copy-start = (bf16[4096,256]{1,0:T(8,128)(2,1)S(1)}, bf16[4096,256]{1,0:T(8,128)(2,1)}, u32[]{:S(2)}) copy-start(bf16[4096,256]{1,0:T(8,128)(2,1)} %get-tuple-element.52) | copy-start | bytes 6291460
  246.7 1.4 copy-start.1
Sparse Core Ops, SparseCore 0:
  10.2 65.2 all-gather.1

commit v6 on v5

--- a/solution.py
+++ b/solution.py
@@ -681,7 +681,13 @@
     pair = device(y=y + 1 - 2 * odd)
     z = p.z
     z_up, z_down = device(z=lax.rem(z + 1, 4)), device(z=lax.rem(z + 3, 4))
-    greet([sib, across, up, down, z_up, z_down])
+    xl = p.xl
+    beside = device(xl=1 - xl)
+    greet([sib, across, up, down, z_up, z_down, beside])
+    moments = r.moment_all
+    here = moments.at[xl * 4 + z]
+    placed = pltpu.make_async_copy(r.moment_own, here, r.store.at[8])
+    placed.start()
     rows, kv = r.rows, r.kv
     block, width = rows.shape[3], rows.shape[4]
     thin = HD // INNER
@@ -761,6 +767,18 @@
     next(kv_ring)
     finish(kv_ring)
     link.start(kv_slots[2], kv.at[other], kv.at[other], sib)
+    placed.wait()
+    moment_slot = link.slot()
+    link.start(moment_slot, here, here, beside)
+    half = r.moment_own.shape[0] // 2
+    parts = lambda ref, i: ref.at[pl.ds(i * half, half)]
+    near_moments = ring_spread(
+        link, z, z_up, z_down, lambda q: moments.at[xl * 4 + q], parts
+    )
+    far_moments = ring_spread(
+        link, z, z_up, z_down, lambda q: moments.at[(1 - xl) * 4 + q], parts
+    )
+    next(near_moments)
     crossed(top_slot, q0, top)
     a_far = spread(1 - xh, top, LOW_FRONT)
     next(a_far)
@@ -782,6 +800,9 @@
     for j in range(INNER):
         r.kv_out[j * thin : (j + 1) * thin, :] = kv[j, :thin, :]
         r.kv_out[HD + j * thin : HD + (j + 1) * thin, :] = kv[j, thin:, :]
+    next(near_moments)
+    link.wait(moment_slot, moments.at[(1 - xl) * 4 + z], beside)
+    next(far_moments)
     project(xh, q0, 0)
     project(xh, q1, 1)
     project(xh, q3, 3)
@@ -794,21 +815,32 @@
     to_sib(sib_slots[1][3], 1 - xh, q3)
     crossed(rest_slots[2], q2, rest)
     to_sib(sib_slots[1][2], 1 - xh, q2)
+    next(far_moments)
+    finish(near_moments)
     project(1 - xh, q1, 5)
     project(1 - xh, q3, 7)
     project(1 - xh, q2, 6)
+    finish(far_moments)
     link.wait(kv_slots[3], r.w_other, sib)
     for copy in stored:
         copy.wait()
     link.drain()
 
 
-def front(tokens, gain, w_query, kv_own, cos, sin):
+def front(tokens, gain, w_query, kv_own, cos, sin, moment_own):
     block, width = tokens.shape
     length = cos.shape[0]
     v = pltpu.VMEM
     shape = jax.ShapeDtypeStruct
-    ins = dict(tokens=tokens, gain=gain, w_query=w_query, kv_own=kv_own, cos=cos, sin=sin)
+    ins = dict(
+        tokens=tokens,
+        gain=gain,
+        w_query=w_query,
+        kv_own=kv_own,
+        cos=cos,
+        sin=sin,
+        moment_own=moment_own,
+    )
     outs = dict(
         query=shape((length, 2 * HD), BF),
         key=shape((length, HD), BF),
@@ -816,21 +848,22 @@
         rows_out=shape((2, 4, 2, block, width), BF),
         w_other=shape(w_query.shape, BF),
         kv_out=shape((2 * HD, width), BF),
+        moment_all=shape((8, *moment_own.shape), BF),
     )
     scratch = dict(
         rows=v((2, 4, 2, block, width), BF),
         kv=v((INNER, 2 * HD // INNER, width), BF),
         acc=v((2 * block, 4 * HD), F32),
-        store=pltpu.SemaphoreType.DMA((8,)),
-        send=pltpu.SemaphoreType.DMA((40,)),
-        recv=pltpu.SemaphoreType.DMA((40,)),
+        store=pltpu.SemaphoreType.DMA((9,)),
+        send=pltpu.SemaphoreType.DMA((48,)),
+        recv=pltpu.SemaphoreType.DMA((48,)),
     )
     whole = pl.BlockSpec(memory_space=pltpu.VMEM)
     far = pl.BlockSpec(memory_space=pl.ANY)
     return pl.pallas_call(
         functools.partial(front_kernel, tuple(ins) + tuple(outs) + tuple(scratch)),
         in_specs=[whole] * len(ins),
-        out_specs=[whole, whole, whole, far, far, whole],
+        out_specs=[whole, whole, whole, far, far, whole, far],
         out_shape=list(outs.values()),
         scratch_shapes=list(scratch.values()),
         compiler_params=pltpu.CompilerParams(
@@ -858,9 +891,8 @@
     moment_kv = jnp.concatenate([moment_key, moment_value], axis=1).T
     halves = jnp.split(moment_kv, 2, axis=1)
     moment_own = jnp.concatenate([moment_query, *halves], axis=0).astype(BF)
-    moment_all = lax.all_gather(moment_own, DP)
-    query, key, value, rows, w_other, w_head = front(
-        tokens[0], gain[None], w_query, kv_own, cos, sin
+    query, key, value, rows, w_other, w_head, moment_all = front(
+        tokens[0], gain[None], w_query, kv_own, cos, sin, moment_own
     )
     length = query.shape[0]
     rows = rows.reshape(length, width)

time: 256 us -> 230 us (0.90)
  between operations: 14.1 us -> 0.7 us
  Pallas kernels: 229 us -> 216 us
    pallas_call x1, Pallas kernels: 103 us -> 85.6 us  [front(): pl.pallas_call(functools.partial(front_kernel, tuple(ins) + tuple(outs) +...]
    pallas_call x1, Pallas kernels: 95.2 us -> 99.4 us  [back(): pl.pallas_call(functools.partial(back_kernel, tuple(ins) + tuple(outs) +...]
  transfers between devices with their start and end apart: 1 -> 0, of which waited for: 0 -> 0; matrix products, arithmetic and copies ran while one was open for 1% -> 0% of each run, Pallas kernels for 52% -> 0%
where the time goes in v6:
time: 230 us
  Pallas kernels  216 us (94%)
  local copies, waits for them, and re-layouts  8.02 us (3%)
  other arithmetic  5.12 us (2%)
    pallas_call x1, Pallas kernels, back(): pl.pallas_call(functools.partial(back_kernel, tuple(ins) + tuple(outs) +...  99.4 us
    pallas_call x1, Pallas kernels, front(): pl.pallas_call(functools.partial(front_kernel, tuple(ins) + tuple(outs) +...  85.6 us
    pallas_call x1, Pallas kernels, attention(): pl.pallas_call(functools.partial(attn_kernel, BQ, TC, HD ** (-0.5)), grid...  31 us

profile of v6, /device:TPU:0, one launch (start us, length us, event | category | flops | bytes accessed | tf_op | source)
XLA Modules:
  0.0 229.9 jit_solution(11893254154597058366)
XLA Ops:
  0.6 0.0 copy-start.2
  0.6 0.0 copy-start.3
  0.7 0.9 fusion
  1.6 1.5 maximum_bitcast_fusion.1.refs_10_
  3.1 1.1 convert.9
  4.2 0.7 pad_maximum_fusion.refs_6_
  5.0 0.0 copy-done.2
  5.0 0.0 copy-done.3
  5.0 0.8 maximum_bitcast_fusion.refs_3_.refs_5_
  5.8 85.6 %front.1 = (bf16[2048,256]{1,0:T(8,128)(2,1)}, bf16[2048,128]{1,0:T(8,128)(2,1)}, bf16[2048,128]{1,0:T(8,128)(2,1)}, bf16[2,4,2,128,4096]{4,3,2,1,0:T(8,128)(2,1...) custom-call(bf16[128,4096]{1,0:T(8,128)(2,1)} %bitcast.23, ...), custom_call_target="tpu_custom_call" | custom-call | tf_op jit(solution)/shard_map/front/pallas_call | solution.py:863
  91.4 31.0 %attention.1 = (bf16[2048,256]{1,0:T(8,128)(2,1)}, bf16[2048,256]{1,0:T(8,128)(2,1)}, bf16[2048,256]{1,0:T(8,128)(2,1)}) custom-call(bf16[2048,256]{1,0:T(8,128)(2,1)} %get-tuple-element.23.q_ref, bf16[2048,128]{1,0:T(8,128)(2,1)} %get-tuple-element.24.k_ref, bf16[2048,128]{1,0:T(8,128)(2,1)} %get-tuple-element.25.v_ref, bf16[2048,256]{1,0:T(8,128)(2,1)} %bitcast.25, ...), custom_call_target="tpu_custom_call" | custom-call | tf_op jit(solution)/shard_map/attention/pallas_call | solution.py:134
  122.4 99.4 %back.1 = (bf16[128,4096]{1,0:T(8,128)(2,1)}, bf16[4096,256]{1,0:T(8,128)(2,1)}, bf16[64,4096]{1,0:T(8,128)(2,1)}, f32[512,256]{1,0:T(8,128)}, f32[64,512]{1,0:T(8,128)}) custom-call(bf16[8,2,128,256]{3,2,1,0:T(8,128)(2,1)} %bitcast.26, bf16[8,2,128,256]{3,2,1,0:T(8,128)(2,1)} %bitcast.27, bf16[4096,256]{1,0:T(8,128)(2,1)} %refs_2_.3, ...), custom_call_target="tpu_custom_call" | custom-call | tf_op jit(solution)/shard_map/back/pallas_call | solution.py:661
  221.9 0.0 copy-start
  221.9 1.7 slice_bitcast_fusion.2
  223.5 1.9 slice_bitcast_fusion
  225.4 2.3 copy.22
  227.7 0.0 copy-done
  227.7 0.0 copy-start.1
  227.7 1.3 copy.23
  229.0 0.1 copy-done.1
  229.1 0.8 copy.24
  (1 shorter events, 0.0 us)
Async XLA Ops:
  0.6 4.3 %copy-start.2 = (bf16[4096,32]{0,1:T(8,128)(2,1)S(1)}, bf16[4096,32]{0,1:T(8,128)(2,1)}, u32[]{:S(2)}) copy-start(bf16[4096,32]{0,1:T(8,128)(2,1)} %param.16) | copy-start | bytes 786436
  0.6 4.3 %copy-start.3 = (bf16[4096,32]{0,1:T(8,128)(2,1)S(1)}, bf16[4096,32]{0,1:T(8,128)(2,1)}, u32[]{:S(2)}) copy-start(bf16[4096,32]{0,1:T(8,128)(2,1)} %param.15) | copy-start | bytes 786436
  221.9 5.8 %copy-start = (bf16[4096,256]{1,0:T(8,128)(2,1)S(1)}, bf16[4096,256]{1,0:T(8,128)(2,1)}, u32[]{:S(2)}) copy-start(bf16[4096,256]{1,0:T(8,128)(2,1)} %get-tuple-element.54) | copy-start | bytes 6291460
  227.7 1.4 copy-start.1
